TPU v7x, 32 devices: a whole 2x2x4 slice. The times are simulated.
32 devices in a mesh: blk: 8 (over z, core), lat: 4 (over y, x).
Axes of the slice: x: 2, y: 2, z: 4, core: 2. Of those that a mesh axis runs over, the one named last changes fastest.
Arguments:
- displacement: float32 [2, 3, 318240], P(None, None, ('blk', 'lat')), may hold values from -5 to 5, as said below
- velocity: float32 [2, 3, 318240], P(None, None, ('blk', 'lat')), may hold values from -2.5 to 2.5, as said below
- lumped_mass: float32 [318240], P(('blk', 'lat')), may hold values from 0.25 to 225, as said below
- shear_modulus: float32 [125, 4096], P(None, ('blk', 'lat')), may hold values from 0.3 to 1
- lame_modulus: float32 [125, 4096], P(None, ('blk', 'lat')), may hold values from 0.3 to 1
- adjoint_sources: bfloat16 [32, 3, 318240], P(None, None, ('blk', 'lat')), may hold values from -24 to 24
- node_numbers: int32 [125, 4096], P(None, ('blk', 'lat')), may hold values from 0 to 9944, as said below
- event_frequency: int32 [2, 32], replicated, may hold values from 0 to 31, each once within a row
Outputs:
- final_displacement: float32 [2, 3, 318240], P(None, None, ('blk', 'lat'))
- final_velocity: float32 [2, 3, 318240], P(None, None, ('blk', 'lat'))
- strain_spectrum: float32 [2, 32, 2, 5, 4096], P(None, None, None, None, ('blk', 'lat'))
Inputs may be any that keep to these rules, and one draw needn't show every extreme that they name: `node_numbers`: each device's columns number its 9945 nodes, each node once across its elements' shared points. A device's element at grid place (ex, ey, ez), 0 <= ex < 2, 0 <= ey < 4, 0 <= ez < 16, touches a neighbour's face when ex or ey is at an end of its range; the first 128 columns of each device are these elements in the order of ex * 4 * 16 + ey * 16 + ez, the remaining columns the other elements in the same order. `event_frequency`: each row gives the events of one supershot distinct frequencies. `displacement`: all copies of a mesh node hold equal values. `velocity`: all copies of a mesh node hold equal values. `lumped_mass`: all copies of a mesh node hold equal values, the mass assembled over all elements of the mesh.
All inputs are finite; a program needn't handle non-finite values.
Results may differ from a plain program's by a relative error of at most 0.0034.
Values sent between devices are 32-bit elements; how exact they have to be, the bound alone decides.
A program may use at most 128 MiB of HBM per device.

v0:
```python
import math

import jax
import jax.numpy as jnp
import numpy as np
from jax import lax
from jax.sharding import PartitionSpec as P

EXB = 2
EYL = 4
EZ = 16
NFREQ = 32
STEP_TOTAL = 4
NXN = 9
NYN = 17
NZN = 65
NODES_DEV = 9945
ELEMS = 128


highest = lax.Precision.HIGHEST


def extended(cells, sides, width, closed):
    for axis, dim in sides:
        count = lax.axis_size(axis)
        ends = count if closed else count - 1
        head = lax.slice_in_dim(cells, 0, width, axis=dim)
        tail = lax.slice_in_dim(cells, cells.shape[dim] - width, cells.shape[dim], axis=dim)
        cells = jnp.concatenate(
            [
                lax.ppermute(tail, axis, [(i, (i + 1) % count) for i in range(ends)]),
                cells,
                lax.ppermute(head, axis, [((i + 1) % count, i) for i in range(ends)]),
            ],
            axis=dim,
        )
    return cells


def gll_tables():
    points = np.array([-1.0, -math.sqrt(3.0 / 7.0), 0.0, math.sqrt(3.0 / 7.0), 1.0])
    weights = np.array([0.1, 49.0 / 90.0, 32.0 / 45.0, 49.0 / 90.0, 0.1])
    products = np.ones(5)
    for target in range(5):
        for source in range(5):
            if source != target:
                products[target] = products[target] * (points[target] - points[source])
    derivative = np.zeros((5, 5))
    for target in range(5):
        for source in range(5):
            if source != target:
                derivative[target, source] = (
                    products[target] / products[source] / (points[target] - points[source])
                )
        derivative[target, target] = -np.sum(derivative[target])
    weight_cube = weights[:, None, None] * weights[None, :, None] * weights[None, None, :] / 8.0
    return (jnp.asarray(derivative, jnp.float32), jnp.asarray(weight_cube, jnp.float32))


def grid_tables():
    elements = np.arange(ELEMS)
    along = elements // (EYL * EZ)
    across = elements // EZ % EYL
    inner = ((along > 0) & (along < EXB - 1) & (across > 0) & (across < EYL - 1)).astype(np.int64)
    order = np.argsort(inner * ELEMS + elements, kind="stable")
    columns_of = np.argsort(order, kind="stable")
    nodes = np.arange(NODES_DEV)
    first = nodes // (NYN * NZN)
    second = nodes // NZN % NYN
    third = nodes % NZN
    elem_x = np.minimum(first // 4, EXB - 1)
    elem_y = np.minimum(second // 4, EYL - 1)
    elem_z = np.minimum(third // 4, EZ - 1)
    point_rows = 25 * (first - 4 * elem_x) + 5 * (second - 4 * elem_y) + (third - 4 * elem_z)
    point_cols = columns_of[(elem_x * EYL + elem_y) * EZ + elem_z]
    return (order, columns_of, point_rows, point_cols)


def source_terms(event_frequency):
    angular_frequencies = jnp.pi * (1.0 + jnp.arange(NFREQ, dtype=jnp.float32)) / (NFREQ + 1.0)
    onehot = (
        event_frequency[:, :, None] == jnp.arange(NFREQ, dtype=jnp.int32)[None, None, :]
    ).astype(jnp.float32)
    selected_entry = jnp.sum(onehot * angular_frequencies[None, None, :], axis=2)
    sample_times = 1.0 + jnp.arange(STEP_TOTAL, dtype=jnp.float32)
    source_pulse = jnp.cos(sample_times[:, None, None] * selected_entry[None, :, :])
    phase_angles = angular_frequencies[:, None] * sample_times[None, :]
    spectra = jnp.stack([jnp.cos(phase_angles), -jnp.sin(phase_angles)])
    return (source_pulse.astype(jnp.bfloat16), spectra)


def spread(values, count):
    lead = values.shape[:-1]
    lower_part = values[..., : 4 * count].reshape(lead + (count, 4))
    upper_part = values[..., 1:].reshape(lead + (count, 4))[..., 3:]
    return jnp.concatenate([lower_part, upper_part], axis=-1)


def fold(values):
    count = values.shape[-2]
    lead = values.shape[:-2]
    lower_part = values[..., :4].reshape(lead + (4 * count,))
    upper_part = jnp.concatenate(
        [jnp.zeros(lead + (count, 3), jnp.float32), values[..., 4:]], axis=-1
    )
    upper_part = upper_part.reshape(lead + (4 * count,))
    single = jnp.zeros(lead + (1,), jnp.float32)
    return jnp.concatenate([lower_part, single], axis=-1) + jnp.concatenate(
        [single, upper_part], axis=-1
    )


def to_elements(field):
    components = field.shape[0]
    values = spread(jnp.moveaxis(field, 1, -1), EXB)
    values = spread(jnp.moveaxis(values, 1, -1), EYL)
    values = spread(jnp.moveaxis(values, 1, -1), EZ)
    values = values.transpose(0, 2, 4, 6, 1, 3, 5)
    return values.reshape(components // 3, 3, 5, 5, 5, ELEMS)


def to_nodes(internal):
    components = internal.shape[0]
    values = internal.reshape(components, 5, 5, 5, EXB, EYL, EZ)
    values = fold(jnp.moveaxis(values, (4, 1), (-2, -1)))
    values = fold(jnp.moveaxis(values, (3, 1), (-2, -1)))
    values = fold(jnp.moveaxis(values, (2, 1), (-2, -1)))
    return values


def element_forces(nodal, shear_pts, lame_pts, derivative, weight_cube):
    shot_count = nodal.shape[0]
    elem_count = nodal.shape[-1]
    grads = (
        2.0 * jnp.einsum("il,scljkn->scijkn", derivative, nodal, precision=highest),
        2.0 * jnp.einsum("jl,scilkn->scijkn", derivative, nodal, precision=highest),
        2.0 * jnp.einsum("kl,scijln->scijkn", derivative, nodal, precision=highest),
    )
    trace = grads[0][:, 0] + grads[1][:, 1] + grads[2][:, 2]
    pressure = lame_pts * trace
    weighted = weight_cube[:, :, :, None]
    forms = ("il,scijkn->scljkn", "jl,scijkn->scilkn", "kl,scijkn->scijln")
    internal = jnp.zeros(nodal.shape, jnp.float32)
    for direction in range(3):
        pieces = []
        for strain_part in range(3):
            stress = shear_pts * (
                grads[direction][:, strain_part] + grads[strain_part][:, direction]
            )
            if strain_part == direction:
                stress = stress + pressure
            pieces.append(weighted * stress)
        flux = jnp.stack(pieces, axis=1)
        internal = internal + jnp.einsum(forms[direction], derivative, flux, precision=highest)
    internal = 2.0 * internal.reshape(3 * shot_count, 125, elem_count)
    third = trace / 3.0
    strains = jnp.stack(
        [
            grads[0][:, 0] - third,
            grads[1][:, 1] - third,
            0.5 * (grads[0][:, 1] + grads[1][:, 0]),
            0.5 * (grads[0][:, 2] + grads[2][:, 0]),
            0.5 * (grads[1][:, 2] + grads[2][:, 1]),
        ],
        axis=1,
    )
    integral = jnp.einsum("sqijkn,ijk->sqn", strains, weight_cube, precision=highest)
    return (internal, integral)


def add_ends(values, axis, lower_plane, upper_plane):
    count = values.shape[axis]
    first_plane = lax.slice_in_dim(values, 0, 1, axis=axis) + jnp.expand_dims(lower_plane, axis)
    middle = lax.slice_in_dim(values, 1, count - 1, axis=axis)
    last_plane = lax.slice_in_dim(values, count - 1, count, axis=axis) + jnp.expand_dims(
        upper_plane, axis
    )
    return jnp.concatenate([first_plane, middle, last_plane], axis=axis)


def assemble(balance):
    components = balance.shape[0]
    cycle_faces = jnp.stack([balance[:, 0], balance[:, -1]], axis=1).reshape(
        components, 2, NYN * NZN
    )
    beside_all = extended(cycle_faces, (("blk", 1),), 1, True)
    from_lower = beside_all[:, 0].reshape(components, NYN, NZN)
    from_upper = beside_all[:, 3].reshape(components, NYN, NZN)
    lat_source = add_ends(balance, 1, from_lower, from_upper)
    lat_faces = jnp.stack([lat_source[:, :, 0], lat_source[:, :, -1]], axis=1).reshape(
        components, 2, NXN * NZN
    )
    lateral = extended(lat_faces, (("lat", 1),), 1, False)
    result = add_ends(
        lat_source,
        2,
        lateral[:, 0].reshape(components, NXN, NZN),
        lateral[:, 3].reshape(components, NXN, NZN),
    )
    return result


def local(
    displacement,
    velocity,
    lumped_mass,
    shear_modulus,
    lame_modulus,
    adjoint_sources,
    node_numbers,
    event_frequency,
):
    shot_count = displacement.shape[0]
    node_count = displacement.shape[2]
    components = 3 * shot_count
    elem_count = node_numbers.shape[1]
    events = adjoint_sources.shape[0]
    derivative, weight_cube = gll_tables()
    source_pulse, spectra = source_terms(event_frequency)
    order, columns_of, point_rows, point_cols = grid_tables()
    grid_nodes = node_numbers[point_rows, point_cols]
    back_order = (
        jnp.zeros((node_count,), jnp.int32)
        .at[grid_nodes]
        .set(jnp.arange(node_count, dtype=jnp.int32))
    )
    grid_shape = (components, NXN, NYN, NZN)
    sources = adjoint_sources.reshape(events * 3, node_count)[:, grid_nodes].reshape(
        events, 3 * node_count
    )
    force_all = jnp.dot(
        source_pulse.reshape(-1, events), sources, preferred_element_type=jnp.float32
    ).reshape((STEP_TOTAL,) + grid_shape)
    motion = displacement.reshape(components, node_count)[:, grid_nodes].reshape(grid_shape)
    speeds = velocity.reshape(components, node_count)[:, grid_nodes].reshape(grid_shape)
    masses = lumped_mass[grid_nodes].reshape(1, NXN, NYN, NZN)
    shear_pts = shear_modulus[:, columns_of].reshape(5, 5, 5, elem_count)
    lame_pts = lame_modulus[:, columns_of].reshape(5, 5, 5, elem_count)
    integrals = []
    for step in range(STEP_TOTAL):
        internal, integral = element_forces(
            to_elements(motion), shear_pts, lame_pts, derivative, weight_cube
        )
        balance = assemble(force_all[step] - to_nodes(internal))
        speeds = speeds + balance / masses
        integrals.append(integral)
        motion = motion + speeds
    stacked = jnp.stack(integrals).reshape(STEP_TOTAL, -1)
    spectrum = jnp.dot(
        spectra.reshape(2 * NFREQ, STEP_TOTAL),
        stacked,
        precision=highest,
        preferred_element_type=jnp.float32,
    ).reshape(2, NFREQ, shot_count, 5, elem_count)
    spectrum = spectrum[..., order]
    final_motion = motion.reshape(components, node_count)[:, back_order]
    final_speeds = speeds.reshape(components, node_count)[:, back_order]
    return (
        final_motion.reshape(shot_count, 3, node_count),
        final_speeds.reshape(shot_count, 3, node_count),
        spectrum,
    )


def solution(mesh):
    return jax.shard_map(
        local,
        mesh=mesh,
        in_specs=(
            P(None, None, ("blk", "lat")),
            P(None, None, ("blk", "lat")),
            P(("blk", "lat")),
            P(None, ("blk", "lat")),
            P(None, ("blk", "lat")),
            P(None, None, ("blk", "lat")),
            P(None, ("blk", "lat")),
            P(),
        ),
        out_specs=(
            P(None, None, ("blk", "lat")),
            P(None, None, ("blk", "lat")),
            P(None, None, None, None, ("blk", "lat")),
        ),
        check_vma=False,
    )
```

profile of v0, /device:TPU:0, one launch (start us, length us, event | category | flops | bytes accessed | tf_op | source)
XLA Modules:
  0.0 815.5 jit_solution(3773652611803178824)
XLA Ops:
  1.5 91.4 %gather_fusion = s32[9945]{0:T(1024)S(1)} fusion(s32[125,128]{1,0:T(8,128)S(1)} %copy-done, s32[9945]{0:T(1024)} %constant.155), kind=kCustom, calls=%fused_computation | custom fusion | bytes 159120 | tf_op jit(solution)/shard_map/gather | solution.py:222
  93.0 46.3 %scatter_custom_fusion = s32[9945]{0:T(1024)S(1)} fusion(s32[9945]{0:T(1024)S(1)} %fusion.83, s32[9945]{0:T(1024)S(1)} %iota.32, s32[]{:T(128)} %constant.17.clone.1), kind=kCustom, calls=%fused_computation.247 | custom fusion | bytes 39784 | tf_op jit(solution)/shard_map/scatter | solution.py:226
  140.1 3.1 copy.880
  143.2 21.7 %gather_fusion.1 = f32[9945,6]{1,0:T(8,128)} fusion(f32[6,9945]{0,1:T(8,128)} %copy.880, s32[10240]{0:T(1024)S(1)} %get-tuple-element.170), kind=kCustom, calls=%fused_computation.1 | custom fusion | bytes 517140 | tf_op jit(solution)/shard_map/gather | solution.py:235
  164.9 3.3 copy.881
  169.8 6.9 reshape.460
  176.7 10.2 %slice.665 = f32[6,2,5,4,5,16,1]{6,5,3,4,2,1,0:T(8,128)} slice(f32[6,2,5,4,5,16,4]{6,5,3,4,2,1,0:T(8,128)} %reshape.460), slice={[0:6], [0:2], [0:5], [0:4], [0:5], [0:16], [3:4]} | slice | bytes 153600 | tf_op jit(solution)/shard_map/slice | solution.py:96
  186.9 9.6 %copy.894 = f32[6,2,5,4,5,16,1]{5,3,6,4,2,1,0:T(4,128)} copy(f32[6,2,5,4,5,16,1]{6,5,3,4,2,1,0:T(8,128)} %slice.665) | data formatting | bytes 153600 | tf_op jit(solution)/shard_map/slice | solution.py:96
  196.5 7.0 reshape.622
  203.6 9.2 %copy.893 = f32[6,2,5,4,5,16,4]{5,3,6,4,2,1,0:T(4,128)S(1)} copy(f32[6,2,5,4,5,16,4]{6,5,4,3,2,1,0:T(8,128)} %reshape.622) | data formatting | bytes 614400 | tf_op jit(solution)/shard_map/reshape | solution.py:95
  216.9 4.0 reshape.461
  233.4 3.8 mul.717
  259.1 4.6 copy.885
  263.7 4.6 reshape.452
  268.3 3.4 copy.886
  271.8 20.8 %gather_fusion.3 = bf16[9945,96]{1,0:T(8,128)(2,1)} fusion(bf16[96,9945]{0,1:T(8,128)(2,1)S(1)} %copy.886, s32[10240]{0:T(1024)S(1)} %get-tuple-element.170), kind=kCustom, calls=%fused_computation.3 | custom fusion | bytes 3858660 | tf_op jit(solution)/shard_map/gather | solution.py:229
  292.6 4.2 copy.887
  296.8 3.3 reshape.453
  304.7 4.5 collective-permute-start.1
  311.2 3.8 collective-permute-start.2
  318.9 3.1 copy.883
  322.1 21.7 %gather_fusion.2 = f32[9945,6]{1,0:T(8,128)} fusion(f32[6,9945]{0,1:T(8,128)} %copy.883, s32[10240]{0:T(1024)S(1)} %get-tuple-element.170), kind=kCustom, calls=%fused_computation.2 | custom fusion | bytes 517140 | tf_op jit(solution)/shard_map/gather | solution.py:236
  343.7 3.3 copy.884
  347.3 51.5 %gather_fusion.6 = f32[9945]{0:T(1024)S(1)} fusion(f32[9945]{0:T(1024)S(1)} %copy-done.2, s32[10240]{0:T(1024)S(1)} %get-tuple-element.170), kind=kCustom, calls=%fused_computation.6 | custom fusion | bytes 119340 | tf_op jit(solution)/shard_map/gather | solution.py:237
  403.0 6.9 reshape.475
  409.9 10.0 %slice.695 = f32[6,2,5,4,5,16,1]{6,5,3,4,2,1,0:T(8,128)} slice(f32[6,2,5,4,5,16,4]{6,5,3,4,2,1,0:T(8,128)} %reshape.475), slice={[0:6], [0:2], [0:5], [0:4], [0:5], [0:16], [3:4]} | slice | bytes 153600 | tf_op jit(solution)/shard_map/slice | solution.py:96
  419.9 9.1 %copy.938 = f32[6,2,5,4,5,16,1]{5,3,6,4,2,1,0:T(4,128)S(1)} copy(f32[6,2,5,4,5,16,1]{6,5,3,4,2,1,0:T(8,128)} %slice.695) | data formatting | bytes 153600 | tf_op jit(solution)/shard_map/slice | solution.py:96
  429.0 8.0 reshape.623
  437.1 10.4 %copy.937 = f32[6,2,5,4,5,16,4]{5,3,6,4,2,1,0:T(4,128)} copy(f32[6,2,5,4,5,16,4]{6,5,4,3,2,1,0:T(8,128)} %reshape.623) | data formatting | bytes 614400 | tf_op jit(solution)/shard_map/reshape | solution.py:95
  452.1 3.8 reshape.476
  462.4 3.8 mul.738
  481.5 3.8 copy.967
  485.2 2.9 copy.968
  495.4 3.5 collective-permute-start.5
  503.9 4.8 collective-permute-start.6
  522.4 7.3 reshape.489
  529.7 10.0 %slice.725 = f32[6,2,5,4,5,16,1]{6,5,3,4,2,1,0:T(8,128)} slice(f32[6,2,5,4,5,16,4]{6,5,3,4,2,1,0:T(8,128)} %reshape.489), slice={[0:6], [0:2], [0:5], [0:4], [0:5], [0:16], [3:4]} | slice | bytes 153600 | tf_op jit(solution)/shard_map/slice | solution.py:96
  539.7 9.1 %copy.976 = f32[6,2,5,4,5,16,1]{5,3,6,4,2,1,0:T(4,128)S(1)} copy(f32[6,2,5,4,5,16,1]{6,5,3,4,2,1,0:T(8,128)} %slice.725) | data formatting | bytes 153600 | tf_op jit(solution)/shard_map/slice | solution.py:96
  548.8 8.0 reshape.624
  556.8 10.4 %copy.975 = f32[6,2,5,4,5,16,4]{5,3,6,4,2,1,0:T(4,128)} copy(f32[6,2,5,4,5,16,4]{6,5,4,3,2,1,0:T(8,128)} %reshape.624) | data formatting | bytes 614400 | tf_op jit(solution)/shard_map/reshape | solution.py:95
  571.8 3.8 reshape.490
  582.1 3.8 mul.759
  601.4 3.8 copy.1005
  605.2 2.9 copy.1006
  610.5 3.0 copy.1008
  615.5 3.5 collective-permute-start.9
  628.0 4.9 collective-permute-start.10
  648.7 6.9 reshape.503
  655.7 10.0 %slice.755 = f32[6,2,5,4,5,16,1]{6,5,3,4,2,1,0:T(8,128)} slice(f32[6,2,5,4,5,16,4]{6,5,3,4,2,1,0:T(8,128)} %reshape.503), slice={[0:6], [0:2], [0:5], [0:4], [0:5], [0:16], [3:4]} | slice | bytes 153600 | tf_op jit(solution)/shard_map/slice | solution.py:96
  665.7 9.1 %copy.1014 = f32[6,2,5,4,5,16,1]{5,3,6,4,2,1,0:T(4,128)S(1)} copy(f32[6,2,5,4,5,16,1]{6,5,3,4,2,1,0:T(8,128)} %slice.755) | data formatting | bytes 153600 | tf_op jit(solution)/shard_map/slice | solution.py:96
  674.8 7.1 reshape.625
  681.9 9.4 %copy.1013 = f32[6,2,5,4,5,16,4]{5,3,6,4,2,1,0:T(4,128)S(1)} copy(f32[6,2,5,4,5,16,4]{6,5,4,3,2,1,0:T(8,128)} %reshape.625) | data formatting | bytes 614400 | tf_op jit(solution)/shard_map/reshape | solution.py:95
  692.6 2.9 reshape.504
  706.5 3.6 mul.780
  731.5 3.5 collective-permute-start.13
  737.7 5.2 collective-permute-start.14
  747.6 3.8 gather_fusion.9
  751.4 3.1 copy.1070
  757.1 3.1 copy.1053
  760.2 21.7 %gather_fusion.8 = f32[9945,6]{1,0:T(8,128)} fusion(f32[6,9945]{0,1:T(8,128)} %copy.1053, s32[10240]{0:T(1024)S(1)} %copy-done.51), kind=kCustom, calls=%fused_computation.8 | custom fusion | bytes 517140 | tf_op jit(solution)/shard_map/gather | solution.py:258
  781.9 3.3 copy.1054
  786.1 3.1 copy.1051
  789.2 21.7 %gather_fusion.7 = f32[9945,6]{1,0:T(8,128)} fusion(f32[6,9945]{0,1:T(8,128)} %copy.1051, s32[10240]{0:T(1024)S(1)} %copy-done.51), kind=kCustom, calls=%fused_computation.7 | custom fusion | bytes 517140 | tf_op jit(solution)/shard_map/gather | solution.py:257
  810.8 3.3 copy.1052
  (493 shorter events, 208.1 us)
Async XLA Ops:
  0.6 139.3 %copy-start.52 = (f32[2,3,9945]{2,0,1:T(2,128)S(1)}, f32[2,3,9945]{2,0,1:T(2,128)}, u32[]{:S(2)}) copy-start(f32[2,3,9945]{2,0,1:T(2,128)} %param.19) | copy-start | bytes 716044
  216.9 4.0 copy-start.20
  223.0 3.8 copy-start.12
  224.1 4.5 copy-start.21
  224.1 5.5 copy-start.62
  226.8 2.9 copy-start.46
  252.3 47.8 %copy-start.63 = (f32[32]{0:T(128)}, f32[32]{0:T(128)S(1)}, u32[]{:S(2)}) copy-start(f32[32]{0:T(128)S(1)} %add_multiply_fusion.12) | copy-start | bytes 388
  252.3 48.0 %copy-start.65 = (f32[4]{0:T(128)}, f32[4]{0:T(128)S(1)}, u32[]{:S(2)}) copy-start(f32[4]{0:T(128)S(1)} %iota_add_fusion) | copy-start | bytes 52
  252.3 4.2 slice-start.4
  292.5 7.6 copy-start.67
  302.4 16.3 %copy-start.53 = (f32[2,3,9945]{2,0,1:T(2,128)S(1)}, f32[2,3,9945]{2,0,1:T(2,128)}, u32[]{:S(2)}) copy-start(f32[2,3,9945]{2,0,1:T(2,128)} %param.20) | copy-start | bytes 716044
  304.2 6.1 collective-permute-start
  304.7 6.1 collective-permute-start.1
  311.0 11.1 %copy-start.30 = (f32[6,1,17,65]{3,2,1,0:T(8,128)}, f32[6,1,17,65]{3,2,1,0:T(8,128)S(1)}, u32[]{:S(2)}) copy-start(f32[6,1,17,65]{3,2,1,0:T(8,128)S(1)} %get-tuple-element.129) | copy-start | bytes 79564
  311.0 11.1 %copy-start.32 = (f32[6,1,17,65]{3,2,1,0:T(8,128)}, f32[6,1,17,65]{3,2,1,0:T(8,128)S(1)}, u32[]{:S(2)}) copy-start(f32[6,1,17,65]{3,2,1,0:T(8,128)S(1)} %get-tuple-element.130) | copy-start | bytes 79564
  311.2 5.2 collective-permute-start.2
  317.4 83.1 %collective-permute-start.3 = (f32[6,1,585]{2,1,0:T(1,128)S(1)}, f32[6,1,585]{2,1,0:T(1,128)S(1)}, u32[]{:S(2)}, u32[]{:S(2)}) collective-permute-start(f32[6,1,585]{2,1,0:T(1,128)S(1)} %stack.73), channel_id=1, source_target_pairs={{1,0},{2,1},{3,2},{5,4},{6,5},{7,6},{9,8},{10,9},{11,10},{13,12},{... | collective-permute-start | bytes 42128 | tf_op jit(solution)/shard_map/ppermute | solution.py:34
  343.7 3.6 copy-start.2
  347.0 51.9 %copy-start.15 = (f32[9945,6]{0,1:T(8,128)}, f32[9945,6]{0,1:T(8,128)S(1)}, u32[]{:S(2)}) copy-start(f32[9945,6]{0,1:T(8,128)S(1)} %copy.884) | copy-start | bytes 716044
  347.3 53.3 %copy-start.31 = (f32[6,1,17,65]{3,2,1,0:T(8,128)S(1)}, f32[6,1,17,65]{3,2,1,0:T(8,128)}, u32[]{:S(2)}) copy-start(f32[6,1,17,65]{3,2,1,0:T(8,128)} %copy-done.30) | copy-start | bytes 79564
  347.3 53.3 %copy-start.33 = (f32[6,1,17,65]{3,2,1,0:T(8,128)S(1)}, f32[6,1,17,65]{3,2,1,0:T(8,128)}, u32[]{:S(2)}) copy-start(f32[6,1,17,65]{3,2,1,0:T(8,128)} %copy-done.32) | copy-start | bytes 79564
  347.3 53.3 %copy-start.55 = (f32[6,9,1,65]{3,2,1,0:T(1,128)S(1)}, f32[6,9,1,65]{3,2,1,0:T(1,128)}, u32[]{:S(2)}) copy-start(f32[6,9,1,65]{3,2,1,0:T(1,128)} %get-tuple-element.49) | copy-start | bytes 42124
  481.5 6.7 slice-start.5
  495.1 17.7 %copy-start.54 = (f32[5,5,5,1,1,1]{0,3,2,1,5,4:T(1,128)S(1)}, f32[5,5,5,1,1,1]{0,3,2,1,5,4:T(1,128)}, u32[]{:S(2)}) copy-start(f32[5,5,5,1,1,1]{0,3,2,1,5,4:T(1,128)} %constant.159) | copy-start | bytes 1504
  495.4 5.1 collective-permute-start.4
  495.4 5.9 collective-permute-start.5
  503.0 11.7 %copy-start.43 = (f32[2,29835]{1,0:T(2,128)S(1)}, f32[2,29835]{1,0:T(2,128)}, u32[]{:S(2)}) copy-start(f32[2,29835]{1,0:T(2,128)} %get-tuple-element.82) | copy-start | bytes 716044
  503.8 14.4 %copy-start.39 = (f32[6,1,17,65]{3,2,1,0:T(8,128)S(1)}, f32[6,1,17,65]{3,2,1,0:T(8,128)}, u32[]{:S(2)}) copy-start(f32[6,1,17,65]{3,2,1,0:T(8,128)} %copy-done.38) | copy-start | bytes 79564
  503.8 14.4 %copy-start.41 = (f32[6,1,17,65]{3,2,1,0:T(8,128)S(1)}, f32[6,1,17,65]{3,2,1,0:T(8,128)}, u32[]{:S(2)}) copy-start(f32[6,1,17,65]{3,2,1,0:T(8,128)} %copy-done.40) | copy-start | bytes 79564
  503.9 6.5 collective-permute-start.6
  511.5 6.5 collective-permute-start.7
  601.4 6.7 slice-start.6
  610.4 8.6 %copy-start.64 = (f32[32]{0:T(128)S(1)}, f32[32]{0:T(128)}, u32[]{:S(2)}) copy-start(f32[32]{0:T(128)} %copy-done.63) | copy-start | bytes 388
  610.5 8.6 %copy-start.66 = (f32[4]{0:T(128)S(1)}, f32[4]{0:T(128)}, u32[]{:S(2)}) copy-start(f32[4]{0:T(128)} %copy-done.65) | copy-start | bytes 52
  610.5 9.3 %copy-start.45 = (f32[5,5,5,128]{3,2,1,0:T(8,128)S(1)}, f32[5,5,5,128]{3,2,1,0:T(8,128)}, u32[]{:S(2)}) copy-start(f32[5,5,5,128]{3,2,1,0:T(8,128)} %copy-done.44) | copy-start | bytes 192004
  610.5 9.3 %copy-start.47 = (f32[5,5,5,128]{3,2,1,0:T(8,128)S(1)}, f32[5,5,5,128]{3,2,1,0:T(8,128)}, u32[]{:S(2)}) copy-start(f32[5,5,5,128]{3,2,1,0:T(8,128)} %copy-done.46) | copy-start | bytes 192004
  610.5 10.6 %copy-start.42 = (f32[2,29835]{1,0:T(2,128)S(1)}, f32[2,29835]{1,0:T(2,128)}, u32[]{:S(2)}) copy-start(f32[2,29835]{1,0:T(2,128)} %get-tuple-element.81) | copy-start | bytes 716044
  615.2 7.2 copy-start.11
  615.4 7.0 collective-permute-start.8
  615.5 7.9 collective-permute-start.9
  622.4 20.4 %copy-start.10 = (f32[6,9,17,65]{3,2,1,0:T(8,128)S(1)}, f32[6,9,17,65]{3,2,1,0:T(8,128)}, u32[]{:S(2)}) copy-start(f32[6,9,17,65]{3,2,1,0:T(8,128)} %get-tuple-element.42) | copy-start | bytes 716044
  625.2 20.3 %copy-start.23 = (f32[9,17,65]{2,1,0:T(8,128)S(1)}, f32[9,17,65]{2,1,0:T(8,128)}, u32[]{:S(2)}) copy-start(f32[9,17,65]{2,1,0:T(8,128)} %copy-done.22) | copy-start | bytes 119344
  628.0 8.4 %collective-permute-start.10 = (f32[6,1,585]{2,1,0:T(1,128)S(1)}, f32[6,1,585]{2,1,0:T(1,128)S(1)}, u32[]{:S(2)}, u32[]{:S(2)}) collective-permute-start(f32[6,1,585]{2,1,0:T(1,128)S(1)} %stack.84), channel_id=1, source_target_pairs={{0,1},{1,2},{2,3},{4,5},{5,6},{6,7},{8,9},{9,10},{10,11},{12,13},{... | collective-permute-start | bytes 42128 | tf_op jit(solution)/shard_map/ppermute | solution.py:32
  638.9 5.6 collective-permute-start.11
  725.5 4.3 copy-start.17
  726.7 3.1 copy-start.18
  729.8 13.1 %copy-start.57 = (f32[1,1280]{1,0:T(1,128)S(1)}, f32[1,1280]{1,0:T(1,128)}, u32[]{:S(2)}) copy-start(f32[1,1280]{1,0:T(1,128)} %stack.182) | copy-start | bytes 15364
  729.8 13.1 %copy-start.58 = (f32[1,1280]{1,0:T(1,128)S(1)}, f32[1,1280]{1,0:T(1,128)}, u32[]{:S(2)}) copy-start(f32[1,1280]{1,0:T(1,128)} %stack.184) | copy-start | bytes 15364
  729.8 13.1 %copy-start.59 = (f32[1,1280]{1,0:T(1,128)S(1)}, f32[1,1280]{1,0:T(1,128)}, u32[]{:S(2)}) copy-start(f32[1,1280]{1,0:T(1,128)} %stack.186) | copy-start | bytes 15364
  731.2 15.1 %copy-start.61 = (f32[1,32,4]{1,2,0:T(4,128)S(1)}, f32[1,32,4]{1,2,0:T(4,128)}, u32[]{:S(2)}) copy-start(f32[1,32,4]{1,2,0:T(4,128)} %get-tuple-element.168) | copy-start | bytes 1540
  731.5 5.6 collective-permute-start.12
  731.5 5.7 collective-permute-start.13
  737.5 8.9 %copy-start.34 = (f32[6,1,17,65]{3,2,1,0:T(8,128)}, f32[6,1,17,65]{3,2,1,0:T(8,128)S(1)}, u32[]{:S(2)}) copy-start(f32[6,1,17,65]{3,2,1,0:T(8,128)S(1)} %get-tuple-element.111) | copy-start | bytes 79564
  737.5 8.9 %copy-start.35 = (f32[6,1,17,65]{3,2,1,0:T(8,128)}, f32[6,1,17,65]{3,2,1,0:T(8,128)S(1)}, u32[]{:S(2)}) copy-start(f32[6,1,17,65]{3,2,1,0:T(8,128)S(1)} %get-tuple-element.112) | copy-start | bytes 79564
  737.5 17.0 %copy-start.19 = (f32[6,9,17,65]{3,2,1,0:T(8,128)S(1)}, f32[6,9,17,65]{3,2,1,0:T(8,128)}, u32[]{:S(2)}) copy-start(f32[6,9,17,65]{3,2,1,0:T(8,128)} %get-tuple-element.36) | copy-start | bytes 716044
  737.7 6.4 collective-permute-start.14
  745.0 9.6 %collective-permute-start.15 = (f32[6,1,585]{2,1,0:T(1,128)S(1)}, f32[6,1,585]{2,1,0:T(1,128)}, u32[]{:S(2)}, u32[]{:S(2)}) collective-permute-start(f32[6,1,585]{2,1,0:T(1,128)S(1)} %stack.179), channel_id=1, source_target_pairs={{1,0},{2,1},{3,2},{5,4},{6,5},{7,6},{9,8},{10,9},{11,10},{13,12},{... | collective-permute-start | bytes 42128 | tf_op jit(solution)/shard_map/ppermute | solution.py:34
  747.6 9.3 %copy-start.14 = (f32[9945,6]{0,1:T(8,128)S(1)}, f32[9945,6]{0,1:T(8,128)}, u32[]{:S(2)}) copy-start(f32[9945,6]{0,1:T(8,128)} %copy-done.13) | copy-start | bytes 716044
  747.6 9.3 %copy-start.16 = (f32[9945,6]{0,1:T(8,128)S(1)}, f32[9945,6]{0,1:T(8,128)}, u32[]{:S(2)}) copy-start(f32[9945,6]{0,1:T(8,128)} %copy-done.15) | copy-start | bytes 716044
  747.6 9.3 %copy-start.28 = (f32[6,9945]{1,0:T(8,128)S(1)}, f32[6,9945]{1,0:T(8,128)}, u32[]{:S(2)}) copy-start(f32[6,9945]{1,0:T(8,128)} %concatenate.199) | copy-start | bytes 716044
  747.6 9.3 %copy-start.50 = (f32[9945]{0:T(1024)S(1)}, f32[9945]{0:T(1024)}, u32[]{:S(2)}) copy-start(f32[9945]{0:T(1024)} %copy-done.49) | copy-start | bytes 119344
  751.4 5.5 copy-start.29
  757.1 3.1 copy-start.51
  810.8 4.2 copy-start.1
  (27 other events, 44.9 us)
where the time goes:
time: 831 us; the launch traced here: 816 us
  local copies, waits for them, and re-layouts  688 us (83%)
  other arithmetic  47.1 us (6%)
  starting transfers between devices  39.7 us (5%)
  matrix products  29.2 us (4%)
    gather x1, local copies, waits for them, and re-layouts, local(): grid_nodes = node_numbers[point_rows, point_cols]  91.4 us
    slice x20, local copies, waits for them, and re-layouts, spread(): upper_part = values[..., 1:].reshape(lead + (count, 4))[..., 3:]  78.4 us
    reshape x8, local copies, waits for them, and re-layouts, spread(): lower_part = values[..., :4 * count].reshape(lead + (count, 4))  69.6 us
    gather x1, local copies, waits for them, and re-layouts, local(): masses = lumped_mass[grid_nodes].reshape(1, NXN, NYN, NZN)  51.5 us
    scatter x1, local copies, waits for them, and re-layouts, local(): back_order = jnp.zeros((node_count,), jnp.int32).at[grid_nodes].set(jnp.a...  46.3 us
    slice x24, local copies, waits for them, and re-layouts, fold(): lower_part = values[..., :4].reshape(lead + (4 * count,))  39.6 us
    unnamed x162, local copies, waits for them, and re-layouts  34 us
    reshape x4, local copies, waits for them, and re-layouts, spread(): upper_part = values[..., 1:].reshape(lead + (count, 4))[..., 3:]  28 us
  transfers between devices with their start and end apart: 16, of which 7 were waited for; matrix products, arithmetic and copies ran while one was open for 13% of the time, Pallas kernels for 0%

commit v1 on v0

v1 whole, which is shorter than its diff:
```python
import functools
import math

import jax
import jax.numpy as jnp
import ml_dtypes
import numpy as np
from jax import lax
from jax.experimental import pallas as pl
from jax.experimental.pallas import tpu as pltpu
from jax.sharding import PartitionSpec as P

EXB = 2
EYL = 4
EZ = 16
NFREQ = 32
STEPS = 4
ELEMS = EXB * EYL * EZ
LANES = 128
ROWS = 208
COMPS = 6
TABLE = 40
FORCE_AT = 16
HALF_X = EYL * EZ
VMEM = pltpu.VMEM
MESH = pl.DeviceIdType.MESH
LIMIT = 56 * 1024 * 1024


def row_of(a, b, c):
    return (5 * a + b) * 8 + c


def gll():
    points = np.array([-1.0, -math.sqrt(3.0 / 7.0), 0.0, math.sqrt(3.0 / 7.0), 1.0])
    weights = np.array([0.1, 49.0 / 90.0, 32.0 / 45.0, 49.0 / 90.0, 0.1])
    products = np.ones(5)
    for i in range(5):
        for j in range(5):
            if i != j:
                products[i] *= points[i] - points[j]
    derivative = np.zeros((5, 5))
    for i in range(5):
        for j in range(5):
            if i != j:
                derivative[i, j] = products[i] / products[j] / (points[i] - points[j])
        derivative[i, i] = -np.sum(derivative[i])
    cube = weights[:, None, None] * weights[None, :, None] * weights[None, None, :] / 8.0
    return derivative, cube


def operators():
    derivative, cube = gll()
    forward = np.zeros((3, ROWS, ROWS))
    weight = np.zeros((ROWS, LANES))
    for a in range(5):
        for b in range(5):
            for c in range(5):
                r = row_of(a, b, c)
                weight[r] = cube[a, b, c]
                for l in range(5):
                    forward[0, r, row_of(l, b, c)] += 2.0 * derivative[a, l]
                    forward[1, r, row_of(a, l, c)] += 2.0 * derivative[b, l]
                    forward[2, r, row_of(a, b, l)] += 2.0 * derivative[c, l]
    backward = forward.transpose(2, 0, 1).reshape(ROWS, 3 * ROWS).copy()
    for d in range(3):
        forward[d, 5] = weight[:, 0] @ forward[d]
    return forward.reshape(3 * ROWS, ROWS), backward, weight.astype(np.float32)


def two_parts(values):
    high = values.astype(np.float32).astype(ml_dtypes.bfloat16)
    low = (values - high.astype(np.float64)).astype(ml_dtypes.bfloat16)
    return jnp.asarray(high), jnp.asarray(low)


def owner_classes():
    every = list(range(ELEMS))
    out = []
    for last_a in (False, True):
        for last_b in (False, True):
            for last_c in (False, True):
                own = [
                    e
                    for e in every
                    if (not last_a or e // HALF_X == EXB - 1)
                    and (not last_b or e // EZ % EYL == EYL - 1)
                    and (not last_c or e % EZ == EZ - 1)
                ]
                out.append((last_a, last_b, last_c, own))
    return out


def over_points(body):
    for last_a, last_b, last_c, own in owner_classes():
        na, nb, nc = (1 if last_a else 4), (1 if last_b else 4), (1 if last_c else 4)

        def step(i, carry, own=own, na=na, nb=nb, nc=nc, la=last_a, lb=last_b, lc=last_c):
            a = 4 if la else i // (nb * nc)
            b = 4 if lb else (i // nc) % nb
            c = 4 if lc else i % nc
            body(25 * a + 5 * b + c, (5 * a + b) * 8 + c, own, (la, lb, lc))
            return carry

        lax.fori_loop(0, na * nb * nc, step, 0)


def lane_parts(shape):
    lane = lax.broadcasted_iota(jnp.int32, shape, len(shape) - 1)
    return lane // HALF_X, lane // EZ % EYL, lane % EZ


def gather_kernel(numbers, values, out, table, stage):
    count = values.shape[1] // LANES

    def turn(i, carry):
        at = pl.multiple_of(i * LANES, LANES)
        block = values[:, pl.ds(at, LANES)]
        full = jnp.concatenate([block, jnp.zeros((LANES - TABLE, LANES), jnp.float32)], axis=0)
        table[pl.ds(at, LANES), :] = full.T
        return carry

    lax.fori_loop(0, count, turn, 0)
    out[...] = jnp.zeros_like(out)
    stage[...] = jnp.zeros_like(stage)
    ex, ey, ez = lane_parts((TABLE, LANES))

    def point(p, row, own, last):
        for e in own:
            stage[pl.ds(e, 1), :] = table[pl.ds(numbers[p, e], 1), :]
        block = stage[...].T[:TABLE]
        keep = None
        for flag, part, top in zip(last, (ex, ey, ez), (EXB - 1, EYL - 1, EZ - 1)):
            if flag:
                keep = (part == top) if keep is None else keep & (part == top)
        if keep is not None:
            block = jnp.where(keep, block, 0.0)
        out[pl.ds(row, TABLE, stride=ROWS), :] = block

    over_points(point)


def local_sum(x):
    x = x.reshape(ROWS // 8, 8, LANES)
    sub = lax.broadcasted_iota(jnp.int32, x.shape, 1)
    ez = lax.broadcasted_iota(jnp.int32, x.shape, 2) % EZ
    turned = pltpu.roll(x, 4, 1)
    x = x + jnp.where((sub == 4) & (ez < EZ - 1), pltpu.roll(turned, LANES - 1, 2), 0.0)
    x = x + jnp.where((sub == 0) & (ez > 0), pltpu.roll(turned, 1, 2), 0.0)
    ex, ey, _ = lane_parts((8, LANES))
    blocks = [x[i] for i in range(ROWS // 8)]
    for a in range(5):
        low, high = blocks[5 * a], blocks[5 * a + 4]
        blocks[5 * a] = low + jnp.where(ey > 0, pltpu.roll(high, EZ, 1), 0.0)
        blocks[5 * a + 4] = high + jnp.where(ey < EYL - 1, pltpu.roll(low, LANES - EZ, 1), 0.0)
    for b in range(5):
        low, high = blocks[b], blocks[20 + b]
        blocks[b] = low + jnp.where(ex > 0, pltpu.roll(high, HALF_X, 1), 0.0)
        blocks[20 + b] = high + jnp.where(ex < EXB - 1, pltpu.roll(low, LANES - HALF_X, 1), 0.0)
    return jnp.concatenate(blocks, axis=0)


def parts(x):
    high = x.astype(jnp.bfloat16)
    return high, (x - high.astype(jnp.float32)).astype(jnp.bfloat16)


def product(left_high, left_low, high, low):
    dot = functools.partial(jnp.dot, preferred_element_type=jnp.float32)
    return dot(left_high, high) + dot(left_high, low) + dot(left_low, high)


def step_kernel(
    n_blk, n_lat,
    gathered, shear, lame, weight, fwd_high, fwd_low, bwd_high, bwd_low,
    state, integrals,
    u, v, force, inverse, shear_w, lame_w, grads, flux_high, flux_low, balance,
    send_x, send_y, recv_x, recv_y, sx, rx, sy, ry,
):
    blk, lat = lax.axis_index("blk"), lax.axis_index("lat")
    up, down = lax.rem(blk + 1, n_blk), lax.rem(blk + n_blk - 1, n_blk)
    has_down, has_up = lat > 0, lat < n_lat - 1
    recv_y[...] = jnp.zeros_like(recv_y)
    barrier = pltpu.get_barrier_semaphore()
    for other in (up, down):
        pl.semaphore_signal(barrier, inc=1, device_id=(other, lat), device_id_type=MESH)

    @pl.when(has_down)
    def _():
        pl.semaphore_signal(barrier, inc=1, device_id=(blk, lat - 1), device_id_type=MESH)

    @pl.when(has_up)
    def _():
        pl.semaphore_signal(barrier, inc=1, device_id=(blk, lat + 1), device_id_type=MESH)

    shear_w[...] = jnp.zeros_like(shear_w)
    lame_w[...] = jnp.zeros_like(lame_w)
    for j in range(25):
        shear_w[8 * j : 8 * j + 5, :] = shear[5 * j : 5 * j + 5, :]
        lame_w[8 * j : 8 * j + 5, :] = lame[5 * j : 5 * j + 5, :]
    shear_w[...] = shear_w[...] * weight[...]
    lame_w[...] = lame_w[...] * weight[...]
    for c in range(COMPS):
        u[:, c * LANES : (c + 1) * LANES] = local_sum(gathered[c])
        v[:, c * LANES : (c + 1) * LANES] = local_sum(gathered[COMPS + c])
    mass = local_sum(gathered[2 * COMPS])
    inverse[...] = 1.0 / jnp.where(mass > 0.0, mass, 1.0)

    def forces(i, carry):
        force[i] = local_sum(gathered[FORCE_AT + i])
        return carry

    lax.fori_loop(0, STEPS * COMPS, forces, 0)

    pl.semaphore_wait(barrier, 2 + jnp.minimum(lat, 1) + jnp.minimum(n_lat - 1 - lat, 1))

    ex40, _, _ = lane_parts((40, LANES))
    _, ey8, _ = lane_parts((8, LANES))

    def cols(c):
        return slice(c * LANES, (c + 1) * LANES)

    def step(k, carry):
        high, low = parts(u[...])
        grads[...] = product(fwd_high[...], fwd_low[...], high, low)
        for s in range(2):
            g = [
                [grads[d * ROWS : (d + 1) * ROWS, cols(3 * s + q)] for q in range(3)]
                for d in range(3)
            ]
            trace = g[0][0] + g[1][1] + g[2][2]
            pressure = lame_w[...] * trace
            for d in range(3):
                for q in range(d, 3):
                    stress = shear_w[...] * (g[d][q] + g[q][d])
                    if d == q:
                        stress = stress + pressure
                    sh, sl = parts(stress)
                    flux_high[d * ROWS : (d + 1) * ROWS, cols(3 * s + q)] = sh
                    flux_low[d * ROWS : (d + 1) * ROWS, cols(3 * s + q)] = sl
                    if d != q:
                        flux_high[q * ROWS : (q + 1) * ROWS, cols(3 * s + d)] = sh
                        flux_low[q * ROWS : (q + 1) * ROWS, cols(3 * s + d)] = sl
            t = [[grads[d * ROWS + 5 : d * ROWS + 6, cols(3 * s + q)] for q in range(3)] for d in range(3)]
            third = (t[0][0] + t[1][1] + t[2][2]) / 3.0
            pieces = (
                t[0][0] - third,
                t[1][1] - third,
                0.5 * (t[0][1] + t[1][0]),
                0.5 * (t[0][2] + t[2][0]),
                0.5 * (t[1][2] + t[2][1]),
            )
            integrals[k, s] = jnp.concatenate(pieces + (jnp.zeros((3, LANES), jnp.float32),), axis=0)
        balance[...] = product(bwd_high[...], bwd_low[...], flux_high[...], flux_low[...])
        for c in range(COMPS):
            balance[:, cols(c)] = force[COMPS * k + c] - local_sum(balance[:, cols(c)])

        for q in range(3):
            low0, low1 = balance[0:40, cols(q)], balance[0:40, cols(3 + q)]
            top0, top1 = balance[160:200, cols(q)], balance[160:200, cols(3 + q)]
            send_x[0, :, cols(q)] = jnp.where(ex40 == 0, low0, pltpu.roll(low1, HALF_X, 1))
            send_x[1, :, cols(q)] = jnp.where(ex40 == 1, top0, pltpu.roll(top1, HALF_X, 1))
        copies = [
            pltpu.make_async_remote_copy(
                src_ref=send_x.at[side], dst_ref=recv_x.at[k, side],
                send_sem=sx.at[k, side], recv_sem=rx.at[k, side],
                device_id=(other, lat), device_id_type=MESH,
            )
            for side, other in ((0, down), (1, up))
        ]
        for copy in copies:
            copy.start()
        for copy in copies:
            copy.wait()
        for q in range(3):
            from_up, from_down = recv_x[k, 0, :, cols(q)], recv_x[k, 1, :, cols(q)]
            for s in range(2):
                c = 3 * s + q
                fd = pltpu.roll(from_down, HALF_X, 1) if s == 0 else from_down
                fu = pltpu.roll(from_up, HALF_X, 1) if s == 0 else from_up
                balance[0:40, cols(c)] = balance[0:40, cols(c)] + jnp.where(ex40 == 0, fd, 0.0)
                balance[160:200, cols(c)] = balance[160:200, cols(c)] + jnp.where(ex40 == 1, fu, 0.0)

        for a in range(5):
            for group in range(2):
                low_pack = jnp.zeros((8, LANES), jnp.float32)
                top_pack = jnp.zeros((8, LANES), jnp.float32)
                for slot in range(min(4, COMPS - 4 * group)):
                    c = 4 * group + slot
                    low_face = balance[40 * a : 40 * a + 8, cols(c)]
                    top_face = balance[40 * a + 32 : 40 * a + 40, cols(c)]
                    if slot:
                        low_face = pltpu.roll(low_face, slot * EZ, 1)
                    if slot < 3:
                        top_face = pltpu.roll(top_face, LANES - (3 - slot) * EZ, 1)
                    low_pack = jnp.where(ey8 == slot, low_face, low_pack)
                    top_pack = jnp.where(ey8 == slot, top_face, top_pack)
                send_y[0, 8 * a : 8 * a + 8, cols(group)] = low_pack
                send_y[1, 8 * a : 8 * a + 8, cols(group)] = top_pack

        to_down = pltpu.make_async_remote_copy(
            src_ref=send_y.at[0], dst_ref=recv_y.at[k, 0],
            send_sem=sy.at[k, 0], recv_sem=ry.at[k, 0],
            device_id=(blk, jnp.maximum(lat - 1, 0)), device_id_type=MESH,
        )
        to_up = pltpu.make_async_remote_copy(
            src_ref=send_y.at[1], dst_ref=recv_y.at[k, 1],
            send_sem=sy.at[k, 1], recv_sem=ry.at[k, 1],
            device_id=(blk, jnp.minimum(lat + 1, n_lat - 1)), device_id_type=MESH,
        )

        @pl.when(has_down)
        def _():
            to_down.start()

        @pl.when(has_up)
        def _():
            to_up.start()

        @pl.when(has_down)
        def _():
            to_down.wait_send()
            to_up.wait_recv()

        @pl.when(has_up)
        def _():
            to_up.wait_send()
            to_down.wait_recv()

        for a in range(5):
            for c in range(COMPS):
                group, slot = c // 4, c % 4
                fd = recv_y[k, 1, 8 * a : 8 * a + 8, cols(group)]
                fu = recv_y[k, 0, 8 * a : 8 * a + 8, cols(group)]
                if slot:
                    fd = pltpu.roll(fd, LANES - slot * EZ, 1)
                if slot < 3:
                    fu = pltpu.roll(fu, (3 - slot) * EZ, 1)
                r = 40 * a
                balance[r : r + 8, cols(c)] = balance[r : r + 8, cols(c)] + jnp.where(ey8 == 0, fd, 0.0)
                balance[r + 32 : r + 40, cols(c)] = balance[r + 32 : r + 40, cols(c)] + jnp.where(
                    ey8 == EYL - 1, fu, 0.0
                )
        for c in range(COMPS):
            speed = v[:, cols(c)] + balance[:, cols(c)] * inverse[...]
            v[:, cols(c)] = speed
            u[:, cols(c)] = u[:, cols(c)] + speed
        return carry

    lax.fori_loop(0, STEPS, step, 0)
    for c in range(COMPS):
        state[c * ROWS : (c + 1) * ROWS, :] = u[:, cols(c)]
        state[(COMPS + c) * ROWS : (COMPS + c + 1) * ROWS, :] = v[:, cols(c)]
    state[2 * COMPS * ROWS :, :] = jnp.zeros((4 * ROWS, LANES), jnp.float32)


def scatter_kernel(numbers, spectra, state, integrals, out_u, out_v, spectrum, table, stage):
    def point(p, row, own, last):
        block = state[pl.ds(row, 16, stride=ROWS), :]
        full = jnp.concatenate([block, jnp.zeros((LANES - 16, LANES), jnp.float32)], axis=0)
        stage[...] = full.T
        for e in own:
            table[pl.ds(numbers[p, e], 1), :] = stage[pl.ds(e, 1), :]

    over_points(point)
    count = out_u.shape[2]

    def emit(at, width):
        block = table[pl.ds(at, LANES), :].T
        for s in range(2):
            out_u[s, :, pl.ds(at, width)] = block[3 * s : 3 * s + 3, :width]
            out_v[s, :, pl.ds(at, width)] = block[COMPS + 3 * s : COMPS + 3 * s + 3, :width]

    def turn(i, carry):
        emit(pl.multiple_of(i * LANES, LANES), LANES)
        return carry

    lax.fori_loop(0, count // LANES, turn, 0)
    if count % LANES:
        emit(count // LANES * LANES, count % LANES)

    def frequency(f, carry):
        for part in range(2):
            for s in range(2):
                total = spectra[part, STEPS * f] * integrals[0, s, 0:5, :]
                for k in range(1, STEPS):
                    total = total + spectra[part, STEPS * f + k] * integrals[k, s, 0:5, :]
                spectrum[part, f, s] = total
        return carry

    lax.fori_loop(0, NFREQ, frequency, 0)


def local(n_blk, n_lat, displacement, velocity, lumped_mass, shear, lame, sources, numbers, event_frequency):
    nodes = displacement.shape[2]
    padded = -(-nodes // LANES) * LANES
    omega = jnp.pi * (1.0 + jnp.arange(NFREQ, dtype=jnp.float32)) / (NFREQ + 1.0)
    onehot = (event_frequency[:, :, None] == jnp.arange(NFREQ, dtype=jnp.int32)[None, None, :])
    chosen = jnp.sum(onehot.astype(jnp.float32) * omega[None, None, :], axis=2)
    times = 1.0 + jnp.arange(STEPS, dtype=jnp.float32)
    pulse = jnp.cos(times[:, None, None] * chosen[None]).astype(jnp.bfloat16)
    phase = omega[:, None] * times[None, :]
    spectra = jnp.stack([jnp.cos(phase), -jnp.sin(phase)]).reshape(2, NFREQ * STEPS)
    force = jnp.einsum(
        "ce,eqn->cqn", pulse.reshape(STEPS * 2, -1), sources, preferred_element_type=jnp.float32
    )
    values = jnp.concatenate(
        [
            displacement.reshape(COMPS, nodes),
            velocity.reshape(COMPS, nodes),
            lumped_mass[None],
            jnp.zeros((3, nodes), jnp.float32),
            force.reshape(STEPS * COMPS, nodes),
        ],
        axis=0,
    )
    values = jnp.pad(values, ((0, 0), (0, padded - nodes)))
    in_smem = pl.BlockSpec(memory_space=pltpu.SMEM)
    in_vmem = pl.BlockSpec(memory_space=VMEM)
    gathered = pl.pallas_call(
        gather_kernel,
        out_shape=jax.ShapeDtypeStruct((TABLE * ROWS, LANES), jnp.float32),
        in_specs=[in_smem, in_vmem],
        out_specs=in_vmem,
        scratch_shapes=[VMEM((padded, LANES), jnp.float32), VMEM((LANES, LANES), jnp.float32)],
        compiler_params=pltpu.CompilerParams(vmem_limit_bytes=LIMIT),
        name="gather_nodes",
    )(numbers, values)
    forward, backward, weight = operators()
    wide = COMPS * LANES
    f32, bf16 = jnp.float32, jnp.bfloat16
    state, integrals = pl.pallas_call(
        functools.partial(step_kernel, n_blk, n_lat),
        out_shape=(
            jax.ShapeDtypeStruct((16 * ROWS, LANES), f32),
            jax.ShapeDtypeStruct((STEPS, 2, 8, LANES), f32),
        ),
        in_specs=[in_vmem] * 8,
        out_specs=(in_vmem, in_vmem),
        scratch_shapes=[
            VMEM((ROWS, wide), f32),
            VMEM((ROWS, wide), f32),
            VMEM((STEPS * COMPS, ROWS, LANES), f32),
            VMEM((ROWS, LANES), f32),
            VMEM((ROWS, LANES), f32),
            VMEM((ROWS, LANES), f32),
            VMEM((3 * ROWS, wide), f32),
            VMEM((3 * ROWS, wide), bf16),
            VMEM((3 * ROWS, wide), bf16),
            VMEM((ROWS, wide), f32),
            VMEM((2, 40, 3 * LANES), f32),
            VMEM((2, 40, 2 * LANES), f32),
            VMEM((STEPS, 2, 40, 3 * LANES), f32),
            VMEM((STEPS, 2, 40, 2 * LANES), f32),
            pltpu.SemaphoreType.DMA((STEPS, 2)),
            pltpu.SemaphoreType.DMA((STEPS, 2)),
            pltpu.SemaphoreType.DMA((STEPS, 2)),
            pltpu.SemaphoreType.DMA((STEPS, 2)),
        ],
        compiler_params=pltpu.CompilerParams(
            vmem_limit_bytes=LIMIT, collective_id=0, has_side_effects=True
        ),
        name="time_steps",
    )(
        gathered.reshape(TABLE, ROWS, LANES), shear, lame, jnp.asarray(weight),
        *two_parts(forward), *two_parts(backward),
    )
    return pl.pallas_call(
        scatter_kernel,
        out_shape=(
            jax.ShapeDtypeStruct(displacement.shape, f32),
            jax.ShapeDtypeStruct(displacement.shape, f32),
            jax.ShapeDtypeStruct((2, NFREQ, 2, 5, LANES), f32),
        ),
        in_specs=[in_smem, in_smem, in_vmem, in_vmem],
        out_specs=(in_vmem,) * 3,
        scratch_shapes=[VMEM((padded, LANES), f32), VMEM((LANES, LANES), f32)],
        compiler_params=pltpu.CompilerParams(vmem_limit_bytes=LIMIT),
        name="scatter_nodes",
    )(numbers, spectra, state, integrals)


def solution(mesh):
    both = ("blk", "lat")
    return jax.shard_map(
        functools.partial(local, mesh.shape["blk"], mesh.shape["lat"]),
        mesh=mesh,
        in_specs=(
            P(None, None, both), P(None, None, both), P(both), P(None, both), P(None, both),
            P(None, None, both), P(None, both), P(),
        ),
        out_specs=(P(None, None, both), P(None, None, both), P(None, None, None, None, both)),
        check_vma=False,
    )
```

time: 831 us -> 141 us (0.17); the launches traced: 816 us -> 141 us
  local copies, waits for them, and re-layouts: 688 us -> 22.4 us
  Pallas kernels: 0 us -> 116 us
  other arithmetic: 47.1 us -> 1.61 us
  starting transfers between devices: 39.7 us -> 0 us
  matrix products: 29.2 us -> 0.47 us
    gather x17 -> x0, local copies, waits for them, and re-layouts: 273 us -> none  [the longest x1 91.4 us: local(): grid_nodes = node_numbers[point_rows, point_cols]]
    reshape x39 -> x3, local copies, waits for them, and re-layouts: 150 us -> 3.1 us  [the longest x1 1.42 us: local(): force.reshape(STEPS * COMPS, nodes)]
    slice x90 -> x0, local copies, waits for them, and re-layouts: 128 us -> none  [the longest x20 78.4 us: spread(): upper_part = values[..., 1:].reshape(lead + (count, 4))[..., 3:]]
    pallas_call x0 -> x3, Pallas kernels: none -> 116 us  [the longest x1 58 us: local(): pl.pallas_call(functools.partial(step_kernel, n_blk, n_lat), out_shape=(j...]
    scatter x1 -> x0, local copies, waits for them, and re-layouts: 46.3 us -> none  [local(): back_order = jnp.zeros((node_count,), jnp.int32).at[grid_nodes].set(jnp.a...]
    ppermute x16 -> x0, starting transfers between devices: 39.7 us -> none  [the longest x8 20.3 us: extended(): lax.ppermute(head, axis, [((i + 1) % count, i) for i in range(ends)])]
    unnamed x162 -> x4, local copies, waits for them, and re-layouts: 34 us -> 2.06 us
    dot_general x30 -> x1, matrix products: 29.2 us -> 0.47 us  [local(): jnp.einsum('ce,eqn->cqn', pulse.reshape(STEPS * 2, -1), sources, preferre...]
  transfers between devices with their start and end apart: 16 -> 0, of which waited for: 7 -> 0; matrix products, arithmetic and copies ran while one was open for 13% -> 0% of each run, Pallas kernels for 0% -> 0%
where the time goes in v1:
time: 141 us
  Pallas kernels  116 us (82%)
  local copies, waits for them, and re-layouts  22.4 us (16%)
  other arithmetic  1.61 us (1%)
    pallas_call x1, Pallas kernels, local(): pl.pallas_call(functools.partial(step_kernel, n_blk, n_lat), out_shape=(j...  58 us
    pallas_call x1, Pallas kernels, local(): pl.pallas_call(gather_kernel, out_shape=jax.ShapeDtypeStruct((TABLE * ROW...  29.2 us
    pallas_call x1, Pallas kernels, local(): pl.pallas_call(scatter_kernel, out_shape=(jax.ShapeDtypeStruct(displaceme...  28.4 us
    concatenate x1, local copies, waits for them, and re-layouts, local(): jnp.concatenate([displacement.reshape(COMPS, nodes), velocity.reshape(COM...  7.99 us
    pallas_call x3, local copies, waits for them, and re-layouts, local(): pl.pallas_call(scatter_kernel, out_shape=(jax.ShapeDtypeStruct(displaceme...  5.5 us

profile of v1, /device:TPU:0, one launch (start us, length us, event | category | flops | bytes accessed | tf_op | source)
XLA Modules:
  0.0 140.8 jit_solution(4825065750808743537)
XLA Ops:
  0.6 0.0 copy-start
  0.7 1.0 select_reduce_fusion
  1.6 0.1 mul.75
  1.7 0.1 mul.76
  1.8 0.1 mul.73
  1.9 0.1 mul.70
  2.0 0.1 mul.71
  2.1 0.6 pad_maximum_fusion.spectra
  2.7 0.8 broadcast_in_dim.4
  3.5 1.0 copy.28
  4.6 0.8 reshape.102
  5.4 1.0 copy.29
  6.4 0.8 reshape.103
  7.3 0.0 copy-done
  7.3 0.5 fusion.1
  7.7 0.5 copy.30
  8.2 1.4 %reshape.104 = f32[24,9945]{1,0:T(8,128)} reshape(f32[8,3,9945]{2,1,0:T(4,128)S(1)} %copy.30) | data formatting | bytes 1909440 | tf_op jit(solution)/shard_map/reshape | solution.py:413
  9.7 0.7 broadcast_in_dim.5
  10.3 8.0 %concatenate.4 = f32[40,9945]{1,0:T(8,128)S(1)} concatenate(f32[6,9945]{1,0:T(8,128)} %reshape.102, f32[6,9945]{1,0:T(8,128)} %reshape.103, f32[1,9945]{1,0:T(1,128)S(1)} %broadcast_in_dim.4, f32[3,9945]{1,0:T(4,128)} %broadcast_in_dim.5, f32[24,9945]{1,0:T(8,128)} %reshape.104), dimensions={0} | concatenate | bytes 3182400 | tf_op jit(solution)/shard_map/concatenate | solution.py:407
  18.3 1.3 pad.4.values
  19.6 29.2 %gather_nodes.1 = f32[8320,128]{1,0:T(8,128)} custom-call(s32[125,128]{1,0:T(8,128)} %numbers.3, f32[40,9984]{1,0:T(8,128)} %pad.4.values), custom_call_target="tpu_custom_call" | custom-call | tf_op jit(solution)/shard_map/gather_nodes/pallas_call | solution.py:420
  48.8 58.0 %time_steps.1 = (f32[3328,128]{1,0:T(8,128)}, f32[4,2,8,128]{3,2,1,0:T(8,128)}) custom-call(f32[40,208,128]{2,1,0:T(8,128)} %bitcast.8, f32[125,128]{1,0:T(8,128)} %shear.1, f32[125,128]{1,0:T(8,128)} %lame.1, f32[208,128]{1,0:T(8,128)} %constant.24.clone.weight, bf16[624,208]{1,0:T(8,128)(2,1)} %constant.25.clone.fwd_high, ...), custom_call_target="tpu_custom_call" | custom-call | tf_op jit(solution)/shard_map/time_steps/pallas_call | solution.py:432
  106.9 28.4 %scatter_nodes.1 = (f32[2,3,9945]{2,1,0:T(4,128)}, f32[2,3,9945]{2,1,0:T(4,128)}, f32[2,32,2,5,128]{4,3,2,1,0:T(8,128)}) custom-call(s32[125,128]{1,0:T(8,128)} %numbers.3, f32[2,128]{1,0:T(2,128)} %pad_maximum_fusion.spectra, f32[3328,128]{1,0:T(8,128)} %get-tuple-element.5.state, f32[4,2,8,128]{3,2,1,0:T(8,128)} %get-tuple-element.6.integrals), custom_call_target="tpu_custom_call" | custom-call | tf_op jit(solution)/shard_map/scatter_nodes/pallas_call | solution.py:468
  135.3 1.8 %copy.31 = f32[2,3,9945]{2,0,1:T(2,128)} copy(f32[2,3,9945]{2,1,0:T(4,128)} %get-tuple-element.13) | data formatting | bytes 477360 | tf_op jit(solution)/shard_map/scatter_nodes/pallas_call | solution.py:468
  137.1 1.8 %copy.32 = f32[2,3,9945]{2,0,1:T(2,128)} copy(f32[2,3,9945]{2,1,0:T(4,128)} %get-tuple-element.14) | data formatting | bytes 477360 | tf_op jit(solution)/shard_map/scatter_nodes/pallas_call | solution.py:468
  138.8 1.9 %copy.33 = f32[2,32,2,5,128]{4,2,3,1,0:T(2,128)} copy(f32[2,32,2,5,128]{4,3,2,1,0:T(8,128)} %get-tuple-element.15) | data formatting | bytes 655360 | tf_op jit(solution)/shard_map/scatter_nodes/pallas_call | solution.py:468
  (5 shorter events, 0.1 us)
Async XLA Ops:
  0.6 6.6 %copy-start = (bf16[32,3,9945]{2,0,1:T(8,128)(2,1)S(1)}, bf16[32,3,9945]{2,0,1:T(8,128)(2,1)}, u32[]{:S(2)}) copy-start(bf16[32,3,9945]{2,0,1:T(8,128)(2,1)} %param.18) | copy-start | bytes 5728324

commit v2 on v1

--- a/solution.py
+++ b/solution.py
@@ -110,24 +110,39 @@
     return lane // HALF_X, lane // EZ % EYL, lane % EZ
 
 
-def gather_kernel(numbers, values, out, table, stage):
-    count = values.shape[1] // LANES
+def in_batches(items, size):
+    return [items[i : i + size] for i in range(0, len(items), size)]
+
+
+def gather_kernel(numbers, u, v, mass, force, out, table, stage):
+    count = u.shape[2]
+    stage[...] = jnp.zeros_like(stage)
+
+    def collect(at, width):
+        cols = pl.ds(at, width)
+        for q in range(3):
+            stage[2 * q : 2 * q + 2, :width] = u[q, :, cols]
+            stage[COMPS + 2 * q : COMPS + 2 * q + 2, :width] = v[q, :, cols]
+            rows = slice(FORCE_AT + 2 * STEPS * q, FORCE_AT + 2 * STEPS * (q + 1))
+            stage[rows, :width] = force[q, :, cols]
+        stage[2 * COMPS : 2 * COMPS + 1, :width] = mass[:, cols]
+        table[pl.ds(at, LANES), :] = stage[...].T
 
     def turn(i, carry):
-        at = pl.multiple_of(i * LANES, LANES)
-        block = values[:, pl.ds(at, LANES)]
-        full = jnp.concatenate([block, jnp.zeros((LANES - TABLE, LANES), jnp.float32)], axis=0)
-        table[pl.ds(at, LANES), :] = full.T
+        collect(pl.multiple_of(i * LANES, LANES), LANES)
         return carry
 
-    lax.fori_loop(0, count, turn, 0)
+    lax.fori_loop(0, count // LANES, turn, 0)
+    if count % LANES:
+        collect(count // LANES * LANES, count % LANES)
     out[...] = jnp.zeros_like(out)
-    stage[...] = jnp.zeros_like(stage)
     ex, ey, ez = lane_parts((TABLE, LANES))
 
     def point(p, row, own, last):
-        for e in own:
-            stage[pl.ds(e, 1), :] = table[pl.ds(numbers[p, e], 1), :]
+        for batch in in_batches(own, 32):
+            found = [table[pl.ds(numbers[p, e], 1), :] for e in batch]
+            for e, line in zip(batch, found):
+                stage[pl.ds(e, 1), :] = line
         block = stage[...].T[:TABLE]
         keep = None
         for flag, part, top in zip(last, (ex, ey, ez), (EXB - 1, EYL - 1, EZ - 1)):
@@ -175,23 +190,26 @@
     gathered, shear, lame, weight, fwd_high, fwd_low, bwd_high, bwd_low,
     state, integrals,
     u, v, force, inverse, shear_w, lame_w, grads, flux_high, flux_low, balance,
-    send_x, send_y, recv_x, recv_y, sx, rx, sy, ry,
+    send_x, send_y, send_c, recv_x, recv_y, recv_c, sx, rx, sy, ry, sc, rc,
 ):
     blk, lat = lax.axis_index("blk"), lax.axis_index("lat")
     up, down = lax.rem(blk + 1, n_blk), lax.rem(blk + n_blk - 1, n_blk)
     has_down, has_up = lat > 0, lat < n_lat - 1
     recv_y[...] = jnp.zeros_like(recv_y)
+    recv_c[...] = jnp.zeros_like(recv_c)
     barrier = pltpu.get_barrier_semaphore()
     for other in (up, down):
         pl.semaphore_signal(barrier, inc=1, device_id=(other, lat), device_id_type=MESH)
 
     @pl.when(has_down)
     def _():
-        pl.semaphore_signal(barrier, inc=1, device_id=(blk, lat - 1), device_id_type=MESH)
+        for other in (blk, up, down):
+            pl.semaphore_signal(barrier, inc=1, device_id=(other, lat - 1), device_id_type=MESH)
 
     @pl.when(has_up)
     def _():
-        pl.semaphore_signal(barrier, inc=1, device_id=(blk, lat + 1), device_id_type=MESH)
+        for other in (blk, up, down):
+            pl.semaphore_signal(barrier, inc=1, device_id=(other, lat + 1), device_id_type=MESH)
 
     shear_w[...] = jnp.zeros_like(shear_w)
     lame_w[...] = jnp.zeros_like(lame_w)
@@ -201,21 +219,25 @@
     shear_w[...] = shear_w[...] * weight[...]
     lame_w[...] = lame_w[...] * weight[...]
     for c in range(COMPS):
-        u[:, c * LANES : (c + 1) * LANES] = local_sum(gathered[c])
-        v[:, c * LANES : (c + 1) * LANES] = local_sum(gathered[COMPS + c])
+        at = 2 * (c % 3) + c // 3
+        u[:, c * LANES : (c + 1) * LANES] = local_sum(gathered[at])
+        v[:, c * LANES : (c + 1) * LANES] = local_sum(gathered[COMPS + at])
     mass = local_sum(gathered[2 * COMPS])
     inverse[...] = 1.0 / jnp.where(mass > 0.0, mass, 1.0)
 
     def forces(i, carry):
-        force[i] = local_sum(gathered[FORCE_AT + i])
+        k, c = i // COMPS, i % COMPS
+        force[i] = local_sum(gathered[FORCE_AT + 2 * STEPS * (c % 3) + 2 * k + c // 3])
         return carry
 
     lax.fori_loop(0, STEPS * COMPS, forces, 0)
 
-    pl.semaphore_wait(barrier, 2 + jnp.minimum(lat, 1) + jnp.minimum(n_lat - 1 - lat, 1))
+    pl.semaphore_wait(barrier, 2 + 3 * jnp.minimum(lat, 1) + 3 * jnp.minimum(n_lat - 1 - lat, 1))
 
     ex40, _, _ = lane_parts((40, LANES))
     _, ey8, _ = lane_parts((8, LANES))
+    slot8 = lax.broadcasted_iota(jnp.int32, (8, LANES), 1) // EZ
+    corner_places = ((0, 0), (32, EYL - 1), (160, EYL * (EXB - 1)), (192, EYL * EXB - 1))
 
     def cols(c):
         return slice(c * LANES, (c + 1) * LANES)
@@ -250,7 +272,8 @@
                 0.5 * (t[0][2] + t[2][0]),
                 0.5 * (t[1][2] + t[2][1]),
             )
-            integrals[k, s] = jnp.concatenate(pieces + (jnp.zeros((3, LANES), jnp.float32),), axis=0)
+            for m in range(5):
+                integrals[k, m, s : s + 1, :] = pieces[m]
         balance[...] = product(bwd_high[...], bwd_low[...], flux_high[...], flux_low[...])
         for c in range(COMPS):
             balance[:, cols(c)] = force[COMPS * k + c] - local_sum(balance[:, cols(c)])
@@ -260,27 +283,6 @@
             top0, top1 = balance[160:200, cols(q)], balance[160:200, cols(3 + q)]
             send_x[0, :, cols(q)] = jnp.where(ex40 == 0, low0, pltpu.roll(low1, HALF_X, 1))
             send_x[1, :, cols(q)] = jnp.where(ex40 == 1, top0, pltpu.roll(top1, HALF_X, 1))
-        copies = [
-            pltpu.make_async_remote_copy(
-                src_ref=send_x.at[side], dst_ref=recv_x.at[k, side],
-                send_sem=sx.at[k, side], recv_sem=rx.at[k, side],
-                device_id=(other, lat), device_id_type=MESH,
-            )
-            for side, other in ((0, down), (1, up))
-        ]
-        for copy in copies:
-            copy.start()
-        for copy in copies:
-            copy.wait()
-        for q in range(3):
-            from_up, from_down = recv_x[k, 0, :, cols(q)], recv_x[k, 1, :, cols(q)]
-            for s in range(2):
-                c = 3 * s + q
-                fd = pltpu.roll(from_down, HALF_X, 1) if s == 0 else from_down
-                fu = pltpu.roll(from_up, HALF_X, 1) if s == 0 else from_up
-                balance[0:40, cols(c)] = balance[0:40, cols(c)] + jnp.where(ex40 == 0, fd, 0.0)
-                balance[160:200, cols(c)] = balance[160:200, cols(c)] + jnp.where(ex40 == 1, fu, 0.0)
-
         for a in range(5):
             for group in range(2):
                 low_pack = jnp.zeros((8, LANES), jnp.float32)
@@ -298,35 +300,85 @@
                 send_y[0, 8 * a : 8 * a + 8, cols(group)] = low_pack
                 send_y[1, 8 * a : 8 * a + 8, cols(group)] = top_pack
 
-        to_down = pltpu.make_async_remote_copy(
-            src_ref=send_y.at[0], dst_ref=recv_y.at[k, 0],
-            send_sem=sy.at[k, 0], recv_sem=ry.at[k, 0],
-            device_id=(blk, jnp.maximum(lat - 1, 0)), device_id_type=MESH,
-        )
-        to_up = pltpu.make_async_remote_copy(
-            src_ref=send_y.at[1], dst_ref=recv_y.at[k, 1],
-            send_sem=sy.at[k, 1], recv_sem=ry.at[k, 1],
-            device_id=(blk, jnp.minimum(lat + 1, n_lat - 1)), device_id_type=MESH,
-        )
+        for corner in range(4):
+            r, home = corner_places[corner]
+            pack = jnp.zeros((8, LANES), jnp.float32)
+            for c in range(COMPS):
+                edge = balance[r : r + 8, cols(c)]
+                shift = (c - home) * EZ % LANES
+                if shift:
+                    edge = pltpu.roll(edge, shift, 1)
+                pack = jnp.where(slot8 == c, edge, pack)
+            send_c[corner] = pack
+
+        def copy(src, dst, ss, rs, other, row):
+            return pltpu.make_async_remote_copy(
+                src_ref=src, dst_ref=dst, send_sem=ss, recv_sem=rs,
+                device_id=(other, row), device_id_type=MESH,
+            )
+
+        rows = (jnp.maximum(lat - 1, 0), jnp.minimum(lat + 1, n_lat - 1))
+        x_copies = [
+            copy(send_x.at[i], recv_x.at[k, i], sx.at[k, i], rx.at[k, i], (down, up)[i], lat)
+            for i in range(2)
+        ]
+        y_copies = [
+            copy(send_y.at[i], recv_y.at[k, i], sy.at[k, i], ry.at[k, i], blk, rows[i])
+            for i in range(2)
+        ]
+        c_copies = [
+            copy(send_c.at[i], recv_c.at[k, i], sc.at[k, i], rc.at[k, i], (down, up)[i // 2], rows[i % 2])
+            for i in range(4)
+        ]
+        to_down = [y_copies[0], c_copies[0], c_copies[2]]
+        to_up = [y_copies[1], c_copies[1], c_copies[3]]
+        for one in x_copies:
+            one.start()
 
         @pl.when(has_down)
         def _():
-            to_down.start()
+            for one in to_down:
+                one.start()
 
         @pl.when(has_up)
         def _():
-            to_up.start()
+            for one in to_up:
+                one.start()
+
+        for c in range(COMPS):
+            speed = v[:, cols(c)] + balance[:, cols(c)] * inverse[...]
+            v[:, cols(c)] = speed
+            u[:, cols(c)] = u[:, cols(c)] + speed
+
+        for one in x_copies:
+            one.wait()
 
         @pl.when(has_down)
         def _():
-            to_down.wait_send()
-            to_up.wait_recv()
+            for one in to_down:
+                one.wait_send()
+            for one in to_up:
+                one.wait_recv()
 
         @pl.when(has_up)
         def _():
-            to_up.wait_send()
-            to_down.wait_recv()
-
+            for one in to_up:
+                one.wait_send()
+            for one in to_down:
+                one.wait_recv()
+
+        def bump(r, size, c, extra):
+            extra = extra * inverse[r : r + size, :]
+            v[r : r + size, cols(c)] = v[r : r + size, cols(c)] + extra
+            u[r : r + size, cols(c)] = u[r : r + size, cols(c)] + extra
+
+        for q in range(3):
+            from_up, from_down = recv_x[k, 0, :, cols(q)], recv_x[k, 1, :, cols(q)]
+            for s in range(2):
+                fd = pltpu.roll(from_down, HALF_X, 1) if s == 0 else from_down
+                fu = pltpu.roll(from_up, HALF_X, 1) if s == 0 else from_up
+                bump(0, 40, 3 * s + q, jnp.where(ex40 == 0, fd, 0.0))
+                bump(160, 40, 3 * s + q, jnp.where(ex40 == 1, fu, 0.0))
         for a in range(5):
             for c in range(COMPS):
                 group, slot = c // 4, c % 4
@@ -336,21 +388,22 @@
                     fd = pltpu.roll(fd, LANES - slot * EZ, 1)
                 if slot < 3:
                     fu = pltpu.roll(fu, (3 - slot) * EZ, 1)
-                r = 40 * a
-                balance[r : r + 8, cols(c)] = balance[r : r + 8, cols(c)] + jnp.where(ey8 == 0, fd, 0.0)
-                balance[r + 32 : r + 40, cols(c)] = balance[r + 32 : r + 40, cols(c)] + jnp.where(
-                    ey8 == EYL - 1, fu, 0.0
-                )
-        for c in range(COMPS):
-            speed = v[:, cols(c)] + balance[:, cols(c)] * inverse[...]
-            v[:, cols(c)] = speed
-            u[:, cols(c)] = u[:, cols(c)] + speed
+                bump(40 * a, 8, c, jnp.where(ey8 == 0, fd, 0.0))
+                bump(40 * a + 32, 8, c, jnp.where(ey8 == EYL - 1, fu, 0.0))
+        for corner in range(4):
+            r, home = corner_places[corner]
+            pack = recv_c[k, 3 - corner]
+            for c in range(COMPS):
+                shift = (home - c) * EZ % LANES
+                edge = pltpu.roll(pack, shift, 1) if shift else pack
+                bump(r, 8, c, jnp.where(slot8 == home, edge, 0.0))
         return carry
 
     lax.fori_loop(0, STEPS, step, 0)
     for c in range(COMPS):
-        state[c * ROWS : (c + 1) * ROWS, :] = u[:, cols(c)]
-        state[(COMPS + c) * ROWS : (COMPS + c + 1) * ROWS, :] = v[:, cols(c)]
+        at = 2 * (c % 3) + c // 3
+        state[at * ROWS : (at + 1) * ROWS, :] = u[:, cols(c)]
+        state[(COMPS + at) * ROWS : (COMPS + at + 1) * ROWS, :] = v[:, cols(c)]
     state[2 * COMPS * ROWS :, :] = jnp.zeros((4 * ROWS, LANES), jnp.float32)
 
 
@@ -359,17 +412,19 @@
         block = state[pl.ds(row, 16, stride=ROWS), :]
         full = jnp.concatenate([block, jnp.zeros((LANES - 16, LANES), jnp.float32)], axis=0)
         stage[...] = full.T
-        for e in own:
-            table[pl.ds(numbers[p, e], 1), :] = stage[pl.ds(e, 1), :]
+        for batch in in_batches(own, 32):
+            lines = [stage[pl.ds(e, 1), :] for e in batch]
+            for e, line in zip(batch, lines):
+                table[pl.ds(numbers[p, e], 1), :] = line
 
     over_points(point)
     count = out_u.shape[2]
 
     def emit(at, width):
         block = table[pl.ds(at, LANES), :].T
-        for s in range(2):
-            out_u[s, :, pl.ds(at, width)] = block[3 * s : 3 * s + 3, :width]
-            out_v[s, :, pl.ds(at, width)] = block[COMPS + 3 * s : COMPS + 3 * s + 3, :width]
+        for q in range(3):
+            out_u[q, :, pl.ds(at, width)] = block[2 * q : 2 * q + 2, :width]
+            out_v[q, :, pl.ds(at, width)] = block[COMPS + 2 * q : COMPS + 2 * q + 2, :width]
 
     def turn(i, carry):
         emit(pl.multiple_of(i * LANES, LANES), LANES)
@@ -381,11 +436,10 @@
 
     def frequency(f, carry):
         for part in range(2):
-            for s in range(2):
-                total = spectra[part, STEPS * f] * integrals[0, s, 0:5, :]
-                for k in range(1, STEPS):
-                    total = total + spectra[part, STEPS * f + k] * integrals[k, s, 0:5, :]
-                spectrum[part, f, s] = total
+            total = spectra[part, STEPS * f] * integrals[0]
+            for k in range(1, STEPS):
+                total = total + spectra[part, STEPS * f + k] * integrals[k]
+            spectrum[part, f] = total
         return carry
 
     lax.fori_loop(0, NFREQ, frequency, 0)
@@ -402,30 +456,21 @@
     phase = omega[:, None] * times[None, :]
     spectra = jnp.stack([jnp.cos(phase), -jnp.sin(phase)]).reshape(2, NFREQ * STEPS)
     force = jnp.einsum(
-        "ce,eqn->cqn", pulse.reshape(STEPS * 2, -1), sources, preferred_element_type=jnp.float32
+        "ce,eqn->qcn", pulse.reshape(STEPS * 2, -1), sources, preferred_element_type=jnp.float32
     )
-    values = jnp.concatenate(
-        [
-            displacement.reshape(COMPS, nodes),
-            velocity.reshape(COMPS, nodes),
-            lumped_mass[None],
-            jnp.zeros((3, nodes), jnp.float32),
-            force.reshape(STEPS * COMPS, nodes),
-        ],
-        axis=0,
-    )
-    values = jnp.pad(values, ((0, 0), (0, padded - nodes)))
     in_smem = pl.BlockSpec(memory_space=pltpu.SMEM)
     in_vmem = pl.BlockSpec(memory_space=VMEM)
     gathered = pl.pallas_call(
         gather_kernel,
         out_shape=jax.ShapeDtypeStruct((TABLE * ROWS, LANES), jnp.float32),
-        in_specs=[in_smem, in_vmem],
+        in_specs=[in_smem] + [in_vmem] * 4,
         out_specs=in_vmem,
         scratch_shapes=[VMEM((padded, LANES), jnp.float32), VMEM((LANES, LANES), jnp.float32)],
         compiler_params=pltpu.CompilerParams(vmem_limit_bytes=LIMIT),
         name="gather_nodes",
-    )(numbers, values)
+    )(
+        numbers, displacement.transpose(1, 0, 2), velocity.transpose(1, 0, 2), lumped_mass[None], force
+    )
     forward, backward, weight = operators()
     wide = COMPS * LANES
     f32, bf16 = jnp.float32, jnp.bfloat16
@@ -433,7 +478,7 @@
         functools.partial(step_kernel, n_blk, n_lat),
         out_shape=(
             jax.ShapeDtypeStruct((16 * ROWS, LANES), f32),
-            jax.ShapeDtypeStruct((STEPS, 2, 8, LANES), f32),
+            jax.ShapeDtypeStruct((STEPS, 5, 2, LANES), f32),
         ),
         in_specs=[in_vmem] * 8,
         out_specs=(in_vmem, in_vmem),
@@ -450,12 +495,16 @@
             VMEM((ROWS, wide), f32),
             VMEM((2, 40, 3 * LANES), f32),
             VMEM((2, 40, 2 * LANES), f32),
+            VMEM((4, 8, LANES), f32),
             VMEM((STEPS, 2, 40, 3 * LANES), f32),
             VMEM((STEPS, 2, 40, 2 * LANES), f32),
+            VMEM((STEPS, 4, 8, LANES), f32),
             pltpu.SemaphoreType.DMA((STEPS, 2)),
             pltpu.SemaphoreType.DMA((STEPS, 2)),
             pltpu.SemaphoreType.DMA((STEPS, 2)),
             pltpu.SemaphoreType.DMA((STEPS, 2)),
+            pltpu.SemaphoreType.DMA((STEPS, 4)),
+            pltpu.SemaphoreType.DMA((STEPS, 4)),
         ],
         compiler_params=pltpu.CompilerParams(
             vmem_limit_bytes=LIMIT, collective_id=0, has_side_effects=True
@@ -465,12 +514,12 @@
         gathered.reshape(TABLE, ROWS, LANES), shear, lame, jnp.asarray(weight),
         *two_parts(forward), *two_parts(backward),
     )
-    return pl.pallas_call(
+    final_u, final_v, spectrum = pl.pallas_call(
         scatter_kernel,
         out_shape=(
-            jax.ShapeDtypeStruct(displacement.shape, f32),
-            jax.ShapeDtypeStruct(displacement.shape, f32),
-            jax.ShapeDtypeStruct((2, NFREQ, 2, 5, LANES), f32),
+            jax.ShapeDtypeStruct((3, 2, nodes), f32),
+            jax.ShapeDtypeStruct((3, 2, nodes), f32),
+            jax.ShapeDtypeStruct((2, NFREQ, 5, 2, LANES), f32),
         ),
         in_specs=[in_smem, in_smem, in_vmem, in_vmem],
         out_specs=(in_vmem,) * 3,
@@ -478,6 +527,11 @@
         compiler_params=pltpu.CompilerParams(vmem_limit_bytes=LIMIT),
         name="scatter_nodes",
     )(numbers, spectra, state, integrals)
+    return (
+        final_u.transpose(1, 0, 2),
+        final_v.transpose(1, 0, 2),
+        spectrum.transpose(0, 1, 3, 2, 4),
+    )
 
 
 def solution(mesh):

time: 141 us -> 113 us (0.80)
  local copies, waits for them, and re-layouts: 22.4 us -> 1.88 us
  Pallas kernels: 116 us -> 107 us
    pallas_call x1, Pallas kernels: 58 us -> 49 us  [local(): pl.pallas_call(functools.partial(step_kernel, n_blk, n_lat), out_shape=(j...]
    concatenate x1 -> x0, local copies, waits for them, and re-layouts: 7.99 us -> none  [local(): jnp.concatenate([displacement.reshape(COMPS, nodes), velocity.reshape(COM...]
    pallas_call x3 -> x0, local copies, waits for them, and re-layouts: 5.5 us -> none  [local(): pl.pallas_call(scatter_kernel, out_shape=(jax.ShapeDtypeStruct(displaceme...]
    reshape x3 -> x0, local copies, waits for them, and re-layouts: 3.1 us -> none  [the longest x1 1.42 us: local(): force.reshape(STEPS * COMPS, nodes)]
    unnamed x4 -> x2, local copies, waits for them, and re-layouts: 2.06 us -> 0.01 us
where the time goes in v2:
time: 113 us
  Pallas kernels  107 us (95%)
  local copies, waits for them, and re-layouts  1.88 us (2%)
  other arithmetic  1.58 us (1%)
  matrix products  1.42 us (1%)
    pallas_call x1, Pallas kernels, local(): pl.pallas_call(functools.partial(step_kernel, n_blk, n_lat), out_shape=(j...  49 us
    pallas_call x1, Pallas kernels, local(): pl.pallas_call(gather_kernel, out_shape=jax.ShapeDtypeStruct((TABLE * ROW...  29.8 us
    pallas_call x1, Pallas kernels, local(): pl.pallas_call(scatter_kernel, out_shape=(jax.ShapeDtypeStruct((3, 2, nod...  28.5 us

profile of v2, /device:TPU:0, one launch (start us, length us, event | category | flops | bytes accessed | tf_op | source)
XLA Modules:
  0.0 112.8 jit_solution(14918562207628416355)
XLA Ops:
  0.6 0.0 copy-start
  0.7 1.0 select_reduce_fusion
  1.6 0.1 mul.75
  1.7 0.1 mul.76
  1.8 0.1 mul.73
  1.9 0.1 mul.70
  2.0 0.1 mul.71
  2.1 0.5 pad_maximum_fusion.spectra
  2.7 1.4 %broadcast_in_dim.2.mass = f32[1,9945]{1,0:T(1,128)} reshape(f32[9945]{0:T(1024)} %param.15) | data formatting | bytes 79560 | tf_op jit(solution)/shard_map/broadcast_in_dim | solution.py:472
  4.1 0.0 copy-done
  4.1 1.4 %convolution_bitcast_fusion.force = f32[3,8,9945]{2,1,0:T(8,128)} fusion(bf16[32,3,9945]{2,0,1:T(8,128)(2,1)S(1)} %copy-done, f32[8,32]{1,0:T(8,128)S(1)} %bitcast.18, f32[8]{0:T(128)S(1)} %mul.76), kind=kOutput, calls=%fused_computation | convolution fusion | flops 15276032 | bytes 2865216 | tf_op jit(solution)/shard_map/ce,eqn->qcn/dot_general | solution.py:458
  5.5 29.8 %gather_nodes.1 = f32[8320,128]{1,0:T(8,128)} custom-call(s32[125,128]{1,0:T(8,128)} %numbers.3, f32[3,2,9945]{2,1,0:T(2,128)} %bitcast.16, f32[3,2,9945]{2,1,0:T(2,128)} %bitcast.17, f32[1,9945]{1,0:T(1,128)} %broadcast_in_dim.2.mass, f32[3,8,9945]{2,1,0:T(8,128)} %convolution_bitcast_fusion.force), custom_call_target="tpu_custom_call" | custom-call | tf_op jit(solution)/shard_map/gather_nodes/pallas_call | solution.py:463
  35.3 49.0 %time_steps.1 = (f32[3328,128]{1,0:T(8,128)}, f32[4,5,2,128]{3,2,1,0:T(2,128)}) custom-call(f32[40,208,128]{2,1,0:T(8,128)} %bitcast.15, f32[125,128]{1,0:T(8,128)} %shear.1, f32[125,128]{1,0:T(8,128)} %lame.1, f32[208,128]{1,0:T(8,128)} %constant.21.clone.weight, bf16[624,208]{1,0:T(8,128)(2,1)} %constant.22.clone.fwd_high, ...), custom_call_target="tpu_custom_call" | custom-call | tf_op jit(solution)/shard_map/time_steps/pallas_call | solution.py:477
  84.3 28.5 %scatter_nodes.1 = (f32[3,2,9945]{2,1,0:T(2,128)}, f32[3,2,9945]{2,1,0:T(2,128)}, f32[2,32,5,2,128]{4,3,2,1,0:T(2,128)}) custom-call(s32[125,128]{1,0:T(8,128)} %numbers.3, f32[2,128]{1,0:T(2,128)} %pad_maximum_fusion.spectra, f32[3328,128]{1,0:T(8,128)} %get-tuple-element.8.state, f32[4,5,2,128]{3,2,1,0:T(2,128)} %get-tuple-element.9.integrals), custom_call_target="tpu_custom_call" | custom-call | tf_op jit(solution)/shard_map/scatter_nodes/pallas_call | solution.py:517
  (5 shorter events, 0.1 us)
Async XLA Ops:
  0.6 3.5 %copy-start = (bf16[32,3,9945]{2,0,1:T(8,128)(2,1)S(1)}, bf16[32,3,9945]{2,0,1:T(8,128)(2,1)}, u32[]{:S(2)}) copy-start(bf16[32,3,9945]{2,0,1:T(8,128)(2,1)} %param.18) | copy-start | bytes 5728324

commit v3 on v2

--- a/solution.py
+++ b/solution.py
@@ -94,15 +94,38 @@
 def over_points(body):
     for last_a, last_b, last_c, own in owner_classes():
         na, nb, nc = (1 if last_a else 4), (1 if last_b else 4), (1 if last_c else 4)
-
-        def step(i, carry, own=own, na=na, nb=nb, nc=nc, la=last_a, lb=last_b, lc=last_c):
-            a = 4 if la else i // (nb * nc)
-            b = 4 if lb else (i // nc) % nb
-            c = 4 if lc else i % nc
-            body(25 * a + 5 * b + c, (5 * a + b) * 8 + c, own, (la, lb, lc))
+        moves = [
+            (x, y, z)
+            for x in range(EXB if last_a else 1)
+            for y in range(EYL if last_b else 1)
+            for z in range(EZ if last_c else 1)
+        ]
+        moves = moves[: na * nb * nc]
+
+        def step(group, carry, own=own, nb=nb, nc=nc, la=last_a, lb=last_b, lc=last_c, moves=moves):
+            members = []
+            for j, move in enumerate(moves):
+                i = group * len(moves) + j
+                a = 4 if la else i // (nb * nc)
+                b = 4 if lb else (i // nc) % nb
+                c = 4 if lc else i % nc
+                members.append((25 * a + 5 * b + c, (5 * a + b) * 8 + c, move))
+            body(members, own, (la, lb, lc))
             return carry
 
-        lax.fori_loop(0, na * nb * nc, step, 0)
+        lax.fori_loop(0, na * nb * nc // len(moves), step, 0)
+
+
+def shift_of(move):
+    return move[0] * HALF_X + move[1] * EZ + move[2]
+
+
+def chosen_lanes(flags, move, parts_of):
+    keep = None
+    for flag, part, top, back in zip(flags, parts_of, (EXB - 1, EYL - 1, EZ - 1), move):
+        if flag:
+            keep = (part == top - back) if keep is None else keep & (part == top - back)
+    return keep
 
 
 def lane_parts(shape):
@@ -126,7 +149,7 @@
             rows = slice(FORCE_AT + 2 * STEPS * q, FORCE_AT + 2 * STEPS * (q + 1))
             stage[rows, :width] = force[q, :, cols]
         stage[2 * COMPS : 2 * COMPS + 1, :width] = mass[:, cols]
-        table[pl.ds(at, LANES), :] = stage[...].T
+        table[pl.ds(at, LANES), :TABLE] = stage[:TABLE, :].T
 
     def turn(i, carry):
         collect(pl.multiple_of(i * LANES, LANES), LANES)
@@ -138,19 +161,19 @@
     out[...] = jnp.zeros_like(out)
     ex, ey, ez = lane_parts((TABLE, LANES))
 
-    def point(p, row, own, last):
-        for batch in in_batches(own, 32):
-            found = [table[pl.ds(numbers[p, e], 1), :] for e in batch]
-            for e, line in zip(batch, found):
-                stage[pl.ds(e, 1), :] = line
-        block = stage[...].T[:TABLE]
-        keep = None
-        for flag, part, top in zip(last, (ex, ey, ez), (EXB - 1, EYL - 1, EZ - 1)):
-            if flag:
-                keep = (part == top) if keep is None else keep & (part == top)
-        if keep is not None:
-            block = jnp.where(keep, block, 0.0)
-        out[pl.ds(row, TABLE, stride=ROWS), :] = block
+    def point(members, own, last):
+        for p, row, move in members:
+            for batch in in_batches(own, 16):
+                found = [table[pl.ds(numbers[p, e], 1), :] for e in batch]
+                for e, line in zip(batch, found):
+                    stage[pl.ds(e - shift_of(move), 1), :] = line
+        block = stage[:, :TABLE].T
+        for p, row, move in members:
+            moved = pltpu.roll(block, shift_of(move), 1) if shift_of(move) else block
+            keep = chosen_lanes(last, (0, 0, 0), (ex, ey, ez))
+            if keep is not None:
+                moved = jnp.where(keep, moved, 0.0)
+            out[pl.ds(row, TABLE, stride=ROWS), :] = moved
 
     over_points(point)
 
@@ -218,10 +241,10 @@
         lame_w[8 * j : 8 * j + 5, :] = lame[5 * j : 5 * j + 5, :]
     shear_w[...] = shear_w[...] * weight[...]
     lame_w[...] = lame_w[...] * weight[...]
-    for c in range(COMPS):
-        at = 2 * (c % 3) + c // 3
-        u[:, c * LANES : (c + 1) * LANES] = local_sum(gathered[at])
-        v[:, c * LANES : (c + 1) * LANES] = local_sum(gathered[COMPS + at])
+    for s in range(2):
+        for q in range(3):
+            u[s, :, q * LANES : (q + 1) * LANES] = local_sum(gathered[2 * q + s])
+            v[s, :, q * LANES : (q + 1) * LANES] = local_sum(gathered[COMPS + 2 * q + s])
     mass = local_sum(gathered[2 * COMPS])
     inverse[...] = 1.0 / jnp.where(mass > 0.0, mass, 1.0)
 
@@ -242,96 +265,93 @@
     def cols(c):
         return slice(c * LANES, (c + 1) * LANES)
 
-    def step(k, carry):
-        high, low = parts(u[...])
-        grads[...] = product(fwd_high[...], fwd_low[...], high, low)
-        for s in range(2):
-            g = [
-                [grads[d * ROWS : (d + 1) * ROWS, cols(3 * s + q)] for q in range(3)]
-                for d in range(3)
-            ]
-            trace = g[0][0] + g[1][1] + g[2][2]
-            pressure = lame_w[...] * trace
-            for d in range(3):
-                for q in range(d, 3):
-                    stress = shear_w[...] * (g[d][q] + g[q][d])
-                    if d == q:
-                        stress = stress + pressure
-                    sh, sl = parts(stress)
-                    flux_high[d * ROWS : (d + 1) * ROWS, cols(3 * s + q)] = sh
-                    flux_low[d * ROWS : (d + 1) * ROWS, cols(3 * s + q)] = sl
-                    if d != q:
-                        flux_high[q * ROWS : (q + 1) * ROWS, cols(3 * s + d)] = sh
-                        flux_low[q * ROWS : (q + 1) * ROWS, cols(3 * s + d)] = sl
-            t = [[grads[d * ROWS + 5 : d * ROWS + 6, cols(3 * s + q)] for q in range(3)] for d in range(3)]
-            third = (t[0][0] + t[1][1] + t[2][2]) / 3.0
-            pieces = (
-                t[0][0] - third,
-                t[1][1] - third,
-                0.5 * (t[0][1] + t[1][0]),
-                0.5 * (t[0][2] + t[2][0]),
-                0.5 * (t[1][2] + t[2][1]),
-            )
-            for m in range(5):
-                integrals[k, m, s : s + 1, :] = pieces[m]
-        balance[...] = product(bwd_high[...], bwd_low[...], flux_high[...], flux_low[...])
-        for c in range(COMPS):
-            balance[:, cols(c)] = force[COMPS * k + c] - local_sum(balance[:, cols(c)])
-
-        for q in range(3):
-            low0, low1 = balance[0:40, cols(q)], balance[0:40, cols(3 + q)]
-            top0, top1 = balance[160:200, cols(q)], balance[160:200, cols(3 + q)]
-            send_x[0, :, cols(q)] = jnp.where(ex40 == 0, low0, pltpu.roll(low1, HALF_X, 1))
-            send_x[1, :, cols(q)] = jnp.where(ex40 == 1, top0, pltpu.roll(top1, HALF_X, 1))
-        for a in range(5):
-            for group in range(2):
-                low_pack = jnp.zeros((8, LANES), jnp.float32)
-                top_pack = jnp.zeros((8, LANES), jnp.float32)
-                for slot in range(min(4, COMPS - 4 * group)):
-                    c = 4 * group + slot
-                    low_face = balance[40 * a : 40 * a + 8, cols(c)]
-                    top_face = balance[40 * a + 32 : 40 * a + 40, cols(c)]
-                    if slot:
-                        low_face = pltpu.roll(low_face, slot * EZ, 1)
-                    if slot < 3:
-                        top_face = pltpu.roll(top_face, LANES - (3 - slot) * EZ, 1)
-                    low_pack = jnp.where(ey8 == slot, low_face, low_pack)
-                    top_pack = jnp.where(ey8 == slot, top_face, top_pack)
-                send_y[0, 8 * a : 8 * a + 8, cols(group)] = low_pack
-                send_y[1, 8 * a : 8 * a + 8, cols(group)] = top_pack
-
-        for corner in range(4):
-            r, home = corner_places[corner]
-            pack = jnp.zeros((8, LANES), jnp.float32)
-            for c in range(COMPS):
-                edge = balance[r : r + 8, cols(c)]
-                shift = (c - home) * EZ % LANES
-                if shift:
-                    edge = pltpu.roll(edge, shift, 1)
-                pack = jnp.where(slot8 == c, edge, pack)
-            send_c[corner] = pack
-
-        def copy(src, dst, ss, rs, other, row):
-            return pltpu.make_async_remote_copy(
-                src_ref=src, dst_ref=dst, send_sem=ss, recv_sem=rs,
-                device_id=(other, row), device_id_type=MESH,
-            )
-
-        rows = (jnp.maximum(lat - 1, 0), jnp.minimum(lat + 1, n_lat - 1))
+    rows = (jnp.maximum(lat - 1, 0), jnp.minimum(lat + 1, n_lat - 1))
+
+    def copy(src, dst, ss, rs, other, row):
+        return pltpu.make_async_remote_copy(
+            src_ref=src, dst_ref=dst, send_sem=ss, recv_sem=rs,
+            device_id=(other, row), device_id_type=MESH,
+        )
+
+    def copies(j, s):
         x_copies = [
-            copy(send_x.at[i], recv_x.at[k, i], sx.at[k, i], rx.at[k, i], (down, up)[i], lat)
+            copy(send_x.at[s, i], recv_x.at[j, i], sx.at[j, i], rx.at[j, i], (down, up)[i], lat)
             for i in range(2)
         ]
         y_copies = [
-            copy(send_y.at[i], recv_y.at[k, i], sy.at[k, i], ry.at[k, i], blk, rows[i])
+            copy(send_y.at[s, i], recv_y.at[j, i], sy.at[j, i], ry.at[j, i], blk, rows[i])
             for i in range(2)
         ]
         c_copies = [
-            copy(send_c.at[i], recv_c.at[k, i], sc.at[k, i], rc.at[k, i], (down, up)[i // 2], rows[i % 2])
+            copy(send_c.at[s, i], recv_c.at[j, i], sc.at[j, i], rc.at[j, i], (down, up)[i // 2], rows[i % 2])
             for i in range(4)
         ]
         to_down = [y_copies[0], c_copies[0], c_copies[2]]
         to_up = [y_copies[1], c_copies[1], c_copies[3]]
+        return x_copies, to_down, to_up
+
+    def compute(j, s):
+        k = j // 2
+        high, low = parts(u[s])
+        grads[...] = product(fwd_high[...], fwd_low[...], high, low)
+        g = [[grads[d * ROWS : (d + 1) * ROWS, cols(q)] for q in range(3)] for d in range(3)]
+        pressure = lame_w[...] * (g[0][0] + g[1][1] + g[2][2])
+        for d in range(3):
+            for q in range(d, 3):
+                stress = shear_w[...] * (g[d][q] + g[q][d])
+                if d == q:
+                    stress = stress + pressure
+                sh, sl = parts(stress)
+                flux_high[d * ROWS : (d + 1) * ROWS, cols(q)] = sh
+                flux_low[d * ROWS : (d + 1) * ROWS, cols(q)] = sl
+                if d != q:
+                    flux_high[q * ROWS : (q + 1) * ROWS, cols(d)] = sh
+                    flux_low[q * ROWS : (q + 1) * ROWS, cols(d)] = sl
+        t = [[grads[d * ROWS + 5 : d * ROWS + 6, cols(q)] for q in range(3)] for d in range(3)]
+        third = (t[0][0] + t[1][1] + t[2][2]) / 3.0
+        pieces = (
+            t[0][0] - third,
+            t[1][1] - third,
+            0.5 * (t[0][1] + t[1][0]),
+            0.5 * (t[0][2] + t[2][0]),
+            0.5 * (t[1][2] + t[2][1]),
+        )
+        for m in range(5):
+            integrals[j, m : m + 1, :] = pieces[m]
+        balance[...] = product(bwd_high[...], bwd_low[...], flux_high[...], flux_low[...])
+        for q in range(3):
+            balance[:, cols(q)] = force[3 * j + q] - local_sum(balance[:, cols(q)])
+
+        low0, low1 = balance[0:40, cols(0)], balance[0:40, cols(1)]
+        top0, top1 = balance[160:200, cols(0)], balance[160:200, cols(1)]
+        send_x[s, 0, :, cols(0)] = jnp.where(ex40 == 0, low0, pltpu.roll(low1, HALF_X, 1))
+        send_x[s, 1, :, cols(0)] = jnp.where(ex40 == 1, top0, pltpu.roll(top1, HALF_X, 1))
+        send_x[s, 0, :, cols(1)] = balance[0:40, cols(2)]
+        send_x[s, 1, :, cols(1)] = pltpu.roll(balance[160:200, cols(2)], HALF_X, 1)
+        for a in range(5):
+            low_pack = balance[40 * a : 40 * a + 8, cols(0)]
+            top_pack = pltpu.roll(balance[40 * a + 32 : 40 * a + 40, cols(0)], LANES - 3 * EZ, 1)
+            for q in range(1, 3):
+                low_face = pltpu.roll(balance[40 * a : 40 * a + 8, cols(q)], q * EZ, 1)
+                top_face = pltpu.roll(
+                    balance[40 * a + 32 : 40 * a + 40, cols(q)], LANES - (3 - q) * EZ, 1
+                )
+                low_pack = jnp.where(ey8 == q, low_face, low_pack)
+                top_pack = jnp.where(ey8 == q, top_face, top_pack)
+            send_y[s, 0, 8 * a : 8 * a + 8, :] = low_pack
+            send_y[s, 1, 8 * a : 8 * a + 8, :] = top_pack
+        for corner in range(4):
+            r, home = corner_places[corner]
+            pack = jnp.zeros((8, LANES), jnp.float32)
+            for q in range(3):
+                edge = balance[r : r + 8, cols(q)]
+                shift = (q - home) * EZ % LANES
+                if shift:
+                    edge = pltpu.roll(edge, shift, 1)
+                pack = jnp.where(slot8 == q, edge, pack)
+            send_c[s, corner] = pack
+
+        x_copies, to_down, to_up = copies(j, s)
         for one in x_copies:
             one.start()
 
@@ -345,11 +365,13 @@
             for one in to_up:
                 one.start()
 
-        for c in range(COMPS):
-            speed = v[:, cols(c)] + balance[:, cols(c)] * inverse[...]
-            v[:, cols(c)] = speed
-            u[:, cols(c)] = u[:, cols(c)] + speed
-
+        for q in range(3):
+            speed = v[s, :, cols(q)] + balance[:, cols(q)] * inverse[...]
+            v[s, :, cols(q)] = speed
+            u[s, :, cols(q)] = u[s, :, cols(q)] + speed
+
+    def finish(j, s):
+        x_copies, to_down, to_up = copies(j, s)
         for one in x_copies:
             one.wait()
 
@@ -367,61 +389,83 @@
             for one in to_down:
                 one.wait_recv()
 
-        def bump(r, size, c, extra):
+        def bump(r, size, q, extra):
             extra = extra * inverse[r : r + size, :]
-            v[r : r + size, cols(c)] = v[r : r + size, cols(c)] + extra
-            u[r : r + size, cols(c)] = u[r : r + size, cols(c)] + extra
-
-        for q in range(3):
-            from_up, from_down = recv_x[k, 0, :, cols(q)], recv_x[k, 1, :, cols(q)]
-            for s in range(2):
-                fd = pltpu.roll(from_down, HALF_X, 1) if s == 0 else from_down
-                fu = pltpu.roll(from_up, HALF_X, 1) if s == 0 else from_up
-                bump(0, 40, 3 * s + q, jnp.where(ex40 == 0, fd, 0.0))
-                bump(160, 40, 3 * s + q, jnp.where(ex40 == 1, fu, 0.0))
+            v[s, r : r + size, cols(q)] = v[s, r : r + size, cols(q)] + extra
+            u[s, r : r + size, cols(q)] = u[s, r : r + size, cols(q)] + extra
+
+        for q in range(3):
+            from_up = recv_x[j, 0, :, cols(q // 2)]
+            from_down = recv_x[j, 1, :, cols(q // 2)]
+            if q == 0:
+                from_down = pltpu.roll(from_down, HALF_X, 1)
+            if q != 1:
+                from_up = pltpu.roll(from_up, HALF_X, 1)
+            bump(0, 40, q, jnp.where(ex40 == 0, from_down, 0.0))
+            bump(160, 40, q, jnp.where(ex40 == 1, from_up, 0.0))
         for a in range(5):
-            for c in range(COMPS):
-                group, slot = c // 4, c % 4
-                fd = recv_y[k, 1, 8 * a : 8 * a + 8, cols(group)]
-                fu = recv_y[k, 0, 8 * a : 8 * a + 8, cols(group)]
-                if slot:
-                    fd = pltpu.roll(fd, LANES - slot * EZ, 1)
-                if slot < 3:
-                    fu = pltpu.roll(fu, (3 - slot) * EZ, 1)
-                bump(40 * a, 8, c, jnp.where(ey8 == 0, fd, 0.0))
-                bump(40 * a + 32, 8, c, jnp.where(ey8 == EYL - 1, fu, 0.0))
+            for q in range(3):
+                fd = recv_y[j, 1, 8 * a : 8 * a + 8, :]
+                fu = pltpu.roll(recv_y[j, 0, 8 * a : 8 * a + 8, :], (3 - q) * EZ, 1)
+                if q:
+                    fd = pltpu.roll(fd, LANES - q * EZ, 1)
+                bump(40 * a, 8, q, jnp.where(ey8 == 0, fd, 0.0))
+                bump(40 * a + 32, 8, q, jnp.where(ey8 == EYL - 1, fu, 0.0))
         for corner in range(4):
             r, home = corner_places[corner]
-            pack = recv_c[k, 3 - corner]
-            for c in range(COMPS):
-                shift = (home - c) * EZ % LANES
+            pack = recv_c[j, 3 - corner]
+            for q in range(3):
+                shift = (home - q) * EZ % LANES
                 edge = pltpu.roll(pack, shift, 1) if shift else pack
-                bump(r, 8, c, jnp.where(slot8 == home, edge, 0.0))
+                bump(r, 8, q, jnp.where(slot8 == home, edge, 0.0))
+
+    def half(j, carry):
+        s = j % 2
+
+        @pl.when(j >= 2)
+        def _():
+            finish(j - 2, s)
+
+        @pl.when(j < 2 * STEPS)
+        def _():
+            compute(j, s)
+
         return carry
 
-    lax.fori_loop(0, STEPS, step, 0)
-    for c in range(COMPS):
-        at = 2 * (c % 3) + c // 3
-        state[at * ROWS : (at + 1) * ROWS, :] = u[:, cols(c)]
-        state[(COMPS + at) * ROWS : (COMPS + at + 1) * ROWS, :] = v[:, cols(c)]
+    lax.fori_loop(0, 2 * STEPS + 2, half, 0)
+    for s in range(2):
+        for q in range(3):
+            at = 2 * q + s
+            state[at * ROWS : (at + 1) * ROWS, :] = u[s, :, cols(q)]
+            state[(COMPS + at) * ROWS : (COMPS + at + 1) * ROWS, :] = v[s, :, cols(q)]
     state[2 * COMPS * ROWS :, :] = jnp.zeros((4 * ROWS, LANES), jnp.float32)
 
 
 def scatter_kernel(numbers, spectra, state, integrals, out_u, out_v, spectrum, table, stage):
-    def point(p, row, own, last):
-        block = state[pl.ds(row, 16, stride=ROWS), :]
-        full = jnp.concatenate([block, jnp.zeros((LANES - 16, LANES), jnp.float32)], axis=0)
-        stage[...] = full.T
-        for batch in in_batches(own, 32):
-            lines = [stage[pl.ds(e, 1), :] for e in batch]
-            for e, line in zip(batch, lines):
-                table[pl.ds(numbers[p, e], 1), :] = line
+    parts_of = lane_parts((16, LANES))
+
+    def point(members, own, last):
+        merged = None
+        for p, row, move in members:
+            block = state[pl.ds(row, 16, stride=ROWS), :]
+            if shift_of(move):
+                block = pltpu.roll(block, LANES - shift_of(move), 1)
+            if merged is None:
+                merged = block
+            else:
+                merged = jnp.where(chosen_lanes(last, move, parts_of), block, merged)
+        stage[:, :16] = merged.T
+        for p, row, move in members:
+            for batch in in_batches(own, 16):
+                lines = [stage[pl.ds(e - shift_of(move), 1), :] for e in batch]
+                for e, line in zip(batch, lines):
+                    table[pl.ds(numbers[p, e], 1), :] = line
 
     over_points(point)
     count = out_u.shape[2]
 
     def emit(at, width):
-        block = table[pl.ds(at, LANES), :].T
+        block = table[pl.ds(at, LANES), :16].T
         for q in range(3):
             out_u[q, :, pl.ds(at, width)] = block[2 * q : 2 * q + 2, :width]
             out_v[q, :, pl.ds(at, width)] = block[COMPS + 2 * q : COMPS + 2 * q + 2, :width]
@@ -436,10 +480,11 @@
 
     def frequency(f, carry):
         for part in range(2):
-            total = spectra[part, STEPS * f] * integrals[0]
-            for k in range(1, STEPS):
-                total = total + spectra[part, STEPS * f + k] * integrals[k]
-            spectrum[part, f] = total
+            for s in range(2):
+                total = spectra[part, STEPS * f] * integrals[s, 0:5, :]
+                for k in range(1, STEPS):
+                    total = total + spectra[part, STEPS * f + k] * integrals[2 * k + s, 0:5, :]
+                spectrum[part, f, :, s, :] = total
         return carry
 
     lax.fori_loop(0, NFREQ, frequency, 0)
@@ -472,19 +517,19 @@
         numbers, displacement.transpose(1, 0, 2), velocity.transpose(1, 0, 2), lumped_mass[None], force
     )
     forward, backward, weight = operators()
-    wide = COMPS * LANES
+    wide = 3 * LANES
     f32, bf16 = jnp.float32, jnp.bfloat16
     state, integrals = pl.pallas_call(
         functools.partial(step_kernel, n_blk, n_lat),
         out_shape=(
             jax.ShapeDtypeStruct((16 * ROWS, LANES), f32),
-            jax.ShapeDtypeStruct((STEPS, 5, 2, LANES), f32),
+            jax.ShapeDtypeStruct((2 * STEPS, 8, LANES), f32),
         ),
         in_specs=[in_vmem] * 8,
         out_specs=(in_vmem, in_vmem),
         scratch_shapes=[
-            VMEM((ROWS, wide), f32),
-            VMEM((ROWS, wide), f32),
+            VMEM((2, ROWS, wide), f32),
+            VMEM((2, ROWS, wide), f32),
             VMEM((STEPS * COMPS, ROWS, LANES), f32),
             VMEM((ROWS, LANES), f32),
             VMEM((ROWS, LANES), f32),
@@ -493,18 +538,18 @@
             VMEM((3 * ROWS, wide), bf16),
             VMEM((3 * ROWS, wide), bf16),
             VMEM((ROWS, wide), f32),
-            VMEM((2, 40, 3 * LANES), f32),
-            VMEM((2, 40, 2 * LANES), f32),
-            VMEM((4, 8, LANES), f32),
-            VMEM((STEPS, 2, 40, 3 * LANES), f32),
-            VMEM((STEPS, 2, 40, 2 * LANES), f32),
-            VMEM((STEPS, 4, 8, LANES), f32),
-            pltpu.SemaphoreType.DMA((STEPS, 2)),
-            pltpu.SemaphoreType.DMA((STEPS, 2)),
-            pltpu.SemaphoreType.DMA((STEPS, 2)),
-            pltpu.SemaphoreType.DMA((STEPS, 2)),
-            pltpu.SemaphoreType.DMA((STEPS, 4)),
-            pltpu.SemaphoreType.DMA((STEPS, 4)),
+            VMEM((2, 2, 40, 2 * LANES), f32),
+            VMEM((2, 2, 40, LANES), f32),
+            VMEM((2, 4, 8, LANES), f32),
+            VMEM((2 * STEPS, 2, 40, 2 * LANES), f32),
+            VMEM((2 * STEPS, 2, 40, LANES), f32),
+            VMEM((2 * STEPS, 4, 8, LANES), f32),
+            pltpu.SemaphoreType.DMA((2 * STEPS, 2)),
+            pltpu.SemaphoreType.DMA((2 * STEPS, 2)),
+            pltpu.SemaphoreType.DMA((2 * STEPS, 2)),
+            pltpu.SemaphoreType.DMA((2 * STEPS, 2)),
+            pltpu.SemaphoreType.DMA((2 * STEPS, 4)),
+            pltpu.SemaphoreType.DMA((2 * STEPS, 4)),
         ],
         compiler_params=pltpu.CompilerParams(
             vmem_limit_bytes=LIMIT, collective_id=0, has_side_effects=True

time: 113 us -> 102 us (0.903)
  Pallas kernels: 107 us -> 95.9 us
    pallas_call x1, Pallas kernels: 49 us -> 42.7 us  [local(): pl.pallas_call(functools.partial(step_kernel, n_blk, n_lat), out_shape=(j...]
    pallas_call x1, Pallas kernels: 28.5 us -> 25 us  [local(): pl.pallas_call(scatter_kernel, out_shape=(jax.ShapeDtypeStruct((3, 2, nod...]
    pallas_call x1, Pallas kernels: 29.8 us -> 28.2 us  [local(): pl.pallas_call(gather_kernel, out_shape=jax.ShapeDtypeStruct((TABLE * ROW...]
where the time goes in v3:
time: 102 us; the launch traced here: 101 us
  Pallas kernels  95.9 us (94%)
  local copies, waits for them, and re-layouts  1.88 us (2%)
  other arithmetic  1.58 us (2%)
  matrix products  1.42 us (1%)
    pallas_call x1, Pallas kernels, local(): pl.pallas_call(functools.partial(step_kernel, n_blk, n_lat), out_shape=(j...  42.7 us
    pallas_call x1, Pallas kernels, local(): pl.pallas_call(gather_kernel, out_shape=jax.ShapeDtypeStruct((TABLE * ROW...  28.2 us
    pallas_call x1, Pallas kernels, local(): pl.pallas_call(scatter_kernel, out_shape=(jax.ShapeDtypeStruct((3, 2, nod...  25 us

profile of v3, /device:TPU:0, one launch (start us, length us, event | category | flops | bytes accessed | tf_op | source)
XLA Modules:
  0.0 101.4 jit_solution(7561178836817438452)
XLA Ops:
  0.6 0.0 copy-start
  0.7 1.0 select_reduce_fusion
  1.6 0.1 mul.75
  1.7 0.1 mul.76
  1.8 0.1 mul.73
  1.9 0.1 mul.70
  2.0 0.1 mul.71
  2.1 0.5 pad_maximum_fusion.spectra
  2.7 1.4 %broadcast_in_dim.2.mass = f32[1,9945]{1,0:T(1,128)} reshape(f32[9945]{0:T(1024)} %param.15) | data formatting | bytes 79560 | tf_op jit(solution)/shard_map/broadcast_in_dim | solution.py:517
  4.1 0.0 copy-done
  4.1 1.4 %convolution_bitcast_fusion.force = f32[3,8,9945]{2,1,0:T(8,128)} fusion(bf16[32,3,9945]{2,0,1:T(8,128)(2,1)S(1)} %copy-done, f32[8,32]{1,0:T(8,128)S(1)} %bitcast.18, f32[8]{0:T(128)S(1)} %mul.76), kind=kOutput, calls=%fused_computation | convolution fusion | flops 15276032 | bytes 2865216 | tf_op jit(solution)/shard_map/ce,eqn->qcn/dot_general | solution.py:503
  5.5 28.2 %gather_nodes.1 = f32[8320,128]{1,0:T(8,128)} custom-call(s32[125,128]{1,0:T(8,128)} %numbers.3, f32[3,2,9945]{2,1,0:T(2,128)} %bitcast.16, f32[3,2,9945]{2,1,0:T(2,128)} %bitcast.17, f32[1,9945]{1,0:T(1,128)} %broadcast_in_dim.2.mass, f32[3,8,9945]{2,1,0:T(8,128)} %convolution_bitcast_fusion.force), custom_call_target="tpu_custom_call" | custom-call | tf_op jit(solution)/shard_map/gather_nodes/pallas_call | solution.py:508
  33.7 42.7 %time_steps.1 = (f32[3328,128]{1,0:T(8,128)}, f32[8,8,128]{2,1,0:T(8,128)}) custom-call(f32[40,208,128]{2,1,0:T(8,128)} %bitcast.15, f32[125,128]{1,0:T(8,128)} %shear.1, f32[125,128]{1,0:T(8,128)} %lame.1, f32[208,128]{1,0:T(8,128)} %constant.21.clone.weight, bf16[624,208]{1,0:T(8,128)(2,1)} %constant.22.clone.fwd_high, ...), custom_call_target="tpu_custom_call" | custom-call | tf_op jit(solution)/shard_map/time_steps/pallas_call | solution.py:522
  76.5 25.0 %scatter_nodes.1 = (f32[3,2,9945]{2,1,0:T(2,128)}, f32[3,2,9945]{2,1,0:T(2,128)}, f32[2,32,5,2,128]{4,3,2,1,0:T(2,128)}) custom-call(s32[125,128]{1,0:T(8,128)} %numbers.3, f32[2,128]{1,0:T(2,128)} %pad_maximum_fusion.spectra, f32[3328,128]{1,0:T(8,128)} %get-tuple-element.8.state, f32[8,8,128]{2,1,0:T(8,128)} %get-tuple-element.9.integrals), custom_call_target="tpu_custom_call" | custom-call | tf_op jit(solution)/shard_map/scatter_nodes/pallas_call | solution.py:562
  (5 shorter events, 0.1 us)
Async XLA Ops:
  0.6 3.5 %copy-start = (bf16[32,3,9945]{2,0,1:T(8,128)(2,1)S(1)}, bf16[32,3,9945]{2,0,1:T(8,128)(2,1)}, u32[]{:S(2)}) copy-start(bf16[32,3,9945]{2,0,1:T(8,128)(2,1)} %param.18) | copy-start | bytes 5728324
